TPU v7x, 256 devices: a whole 4x4x8 slice. The times are simulated.
256 devices in a mesh: dp: 8 (over x, z_hi), seq: 32 (over y, z_lo, core).
Axes of the slice: x: 4, y: 4, z: 8 (z_hi: 2, z_lo: 4; z = z_hi * 4 + z_lo), core: 2. Of those that a mesh axis runs over, the one named last changes fastest.
Arguments:
- tokens: bfloat16 [8, 8192, 1536], P('dp', 'seq'), may hold values from -6 to 6
- pair_in: bfloat16 [8, 512, 512, 128], P('dp', 'seq'), may hold values from -6 to 6
- cotangent: bfloat16 [8, 512, 512, 128], P('dp', 'seq'), may hold values from -6 to 6
- kernel: bfloat16 [32, 1536], replicated, may hold values from -1 to 1
- norm_gain: float32 [1536], replicated, may hold values from 0.1 to 1.9
- left_weight: bfloat16 [1536, 128], replicated, may hold values from -0.15625 to 0.15625
- right_weight: bfloat16 [1536, 128], replicated, may hold values from -0.15625 to 0.15625
- transition_a: bfloat16 [128, 512], replicated, may hold values from -0.5 to 0.5
- transition_b: bfloat16 [512, 128], replicated, may hold values from -0.25 to 0.25
Outputs:
- grad_tokens: bfloat16 [8, 8192, 1536], P('dp', 'seq')
- grad_pair: bfloat16 [8, 512, 512, 128], P('dp', 'seq')
- grad_left_w: float32 [1536, 128], replicated
- grad_right_w: float32 [1536, 128], replicated
- grad_kernel: float32 [32, 1536], replicated
- grad_gain: float32 [1536], replicated
- grad_wa: float32 [128, 512], replicated
- grad_wb: float32 [512, 128], replicated
All inputs are finite; a program needn't handle non-finite values.
Results may differ from a plain program's by a relative error of at most 0.02.
Values may be sent and summed in bfloat16 or wider, within the bound.
A program may use at most 64 MiB of HBM per device.

v0:
```python
import math

import jax
import jax.numpy as jnp
from jax import lax
from jax.sharding import PartitionSpec as P

POOL = 16


def extended_2(array, sides, width):
    for axis, dim in sides:
        devices, length = (lax.axis_size(axis), array.shape[dim])
        up = [(i, (i + 1) % devices) for i in range(devices - 1)]
        down = [(j, i) for i, j in up]
        last = lax.slice_in_dim(array, length - width, length, axis=dim)
        leading = lax.slice_in_dim(array, 0, width, axis=dim)
        before = lax.ppermute(last, axis, up)
        after = lax.ppermute(leading, axis, down)
        array = jnp.concatenate([before, array, after], axis=dim)
    return array


def rms_scale(pooled, norm_gain):
    inverse = lax.rsqrt(jnp.mean(pooled * pooled, axis=-1, keepdims=True) + 1e-06)
    return pooled * inverse * norm_gain


def contract_rows(first_arr, second_arr):
    return lax.dot_general(
        first_arr, second_arr, (((0,), (0,)), ((), ())), preferred_element_type=jnp.float32
    )


def pool_tokens(padded, kernel, seq_tokens):
    channels = padded.shape[-1]
    front_taps = padded[:seq_tokens].astype(jnp.float32).reshape(-1, POOL, channels)
    back_taps = padded[POOL : POOL + seq_tokens].astype(jnp.float32).reshape(-1, POOL, channels)
    kernel_f = kernel.astype(jnp.float32)
    pooled = jnp.sum(front_taps * kernel_f[:POOL], axis=1) + jnp.sum(
        back_taps * kernel_f[POOL:], axis=1
    )
    return (pooled, front_taps, back_taps)


def make_sym(pair_rows, pair_cols, left_rows, right_rows, left_all, right_all):
    outer = left_rows.astype(jnp.float32)[:, None, :] * right_all.astype(jnp.float32)[None]
    outer = outer + right_rows.astype(jnp.float32)[:, None, :] * left_all.astype(jnp.float32)[None]
    return (pair_rows.astype(jnp.float32) + pair_cols.astype(jnp.float32) + outer).astype(
        jnp.bfloat16
    )


def transition_back(sym_rows, cot_rows, transition_a, transition_b):
    preact = jnp.dot(sym_rows, transition_a, preferred_element_type=jnp.float32)
    sigmoid_pre = jax.nn.sigmoid(preact)
    grad_act = jnp.dot(cot_rows, transition_b.T, preferred_element_type=jnp.float32)
    grad_pre = (grad_act * sigmoid_pre * (1.0 + preact * (1.0 - sigmoid_pre))).astype(jnp.bfloat16)
    grad_sym = cot_rows.astype(jnp.float32) + jnp.dot(
        grad_pre, transition_a.T, preferred_element_type=jnp.float32
    )
    activation = (preact * sigmoid_pre).astype(jnp.bfloat16)
    return (grad_sym, contract_rows(sym_rows, grad_pre), contract_rows(activation, cot_rows))


def spread_back(extended, kernel, pair_count):
    kernel_f = kernel.astype(jnp.float32)
    grad_f = extended.astype(jnp.float32)
    half_pool = POOL // 2
    lower_half = (
        grad_f[1 : pair_count + 1, None] * kernel_f[half_pool:POOL]
        + grad_f[0:pair_count, None] * kernel_f[POOL + half_pool :]
    )
    upper_half = (
        grad_f[2 : pair_count + 2, None] * kernel_f[:half_pool]
        + grad_f[1 : pair_count + 1, None] * kernel_f[POOL : POOL + half_pool]
    )
    joined = jnp.concatenate([lower_half, upper_half], axis=1)
    return joined.reshape(pair_count * POOL, -1).astype(jnp.bfloat16)


def kernel_grad(grad_pooled, front_taps, back_taps):
    grad_f = grad_pooled.astype(jnp.float32)[:, None]
    return jnp.concatenate(
        [jnp.sum(grad_f * front_taps, axis=0), jnp.sum(grad_f * back_taps, axis=0)], axis=0
    )


def local(
    tokens,
    pair_in,
    cotangent,
    kernel,
    norm_gain,
    left_weight,
    right_weight,
    transition_a,
    transition_b,
):
    seq_tokens = tokens.shape[1]
    half_pool = POOL // 2
    padded = extended_2(tokens, (("seq", 1),), half_pool)[0]
    pooled, front_taps, back_taps = pool_tokens(padded, kernel, seq_tokens)
    normed_f, norm_back = jax.vjp(rms_scale, pooled, norm_gain)
    normed = normed_f.astype(jnp.bfloat16)
    left_proj = jnp.dot(normed, left_weight, preferred_element_type=jnp.float32).astype(
        jnp.bfloat16
    )
    right_proj = jnp.dot(normed, right_weight, preferred_element_type=jnp.float32).astype(
        jnp.bfloat16
    )
    left_all, right_all = (
        lax.all_gather(left_proj, "seq", axis=0, tiled=True),
        lax.all_gather(right_proj, "seq", axis=0, tiled=True),
    )
    pair_rows = pair_in[0]
    cot_rows = cotangent[0]
    my_rows, plen, pair_channels = pair_rows.shape
    pair_cols = jnp.swapaxes(
        lax.all_to_all(pair_in, "seq", split_axis=2, concat_axis=1, tiled=True)[0], 0, 1
    )
    sym = make_sym(pair_rows, pair_cols, left_proj, right_proj, left_all, right_all)
    block_rows = math.gcd(my_rows, max(1, 2048 // plen))
    count = my_rows // block_rows
    sym_blocks = sym.reshape(count, block_rows * plen, pair_channels)
    cot_blocks = cot_rows.reshape(count, block_rows * plen, pair_channels)

    def add_block(totals, operands):
        grad_sym, grad_wa, grad_wb = transition_back(
            operands[0], operands[1], transition_a, transition_b
        )
        return ((totals[0] + grad_wa, totals[1] + grad_wb), grad_sym.astype(jnp.bfloat16))

    zero_wa = jnp.zeros(transition_a.shape, jnp.float32)
    zero_wb = jnp.zeros(transition_b.shape, jnp.float32)
    (wa_total, wb_total), grad_sym = lax.scan(
        add_block, (zero_wa, zero_wb), (sym_blocks, cot_blocks)
    )
    grad_sym = grad_sym.reshape(my_rows, plen, pair_channels)
    mirrored = jnp.swapaxes(
        lax.all_to_all(grad_sym[None], "seq", split_axis=2, concat_axis=1, tiled=True)[0], 0, 1
    )
    grad_full = grad_sym.astype(jnp.float32) + mirrored.astype(jnp.float32)
    grad_left = jnp.sum(grad_full * right_all.astype(jnp.float32)[None], axis=1).astype(
        jnp.bfloat16
    )
    partial_right = jnp.sum(grad_full * left_proj.astype(jnp.float32)[:, None], axis=0)
    grad_right = lax.psum_scatter(partial_right, "seq", scatter_dimension=0, tiled=True).astype(
        jnp.bfloat16
    )
    grad_normed = jnp.dot(grad_left, left_weight.T, preferred_element_type=jnp.float32) + jnp.dot(
        grad_right, right_weight.T, preferred_element_type=jnp.float32
    )
    grad_pooled_f, grad_gain = norm_back(grad_normed)
    grad_pooled = grad_pooled_f.astype(jnp.bfloat16)
    extended = extended_2(grad_pooled, (("seq", 0),), 1)
    grad_tokens = spread_back(extended, kernel, my_rows)
    grad_kern = kernel_grad(grad_pooled, front_taps, back_taps)
    grad_scale = 1.0 / math.sqrt(lax.axis_size("dp") * plen * plen)
    summed = lax.psum(
        (
            contract_rows(normed, grad_left) * grad_scale,
            contract_rows(normed, grad_right) * grad_scale,
            grad_kern * grad_scale,
            grad_gain * grad_scale,
            wa_total * grad_scale,
            wb_total * grad_scale,
        ),
        ("dp", "seq"),
    )
    return (
        grad_tokens[None],
        grad_full.astype(jnp.bfloat16)[None],
        summed[0],
        summed[1],
        summed[2],
        summed[3],
        summed[4],
        summed[5],
    )


def solution(mesh):
    placed = (
        P("dp", "seq", None),
        P("dp", "seq", None, None),
        P("dp", "seq", None, None),
        P(),
        P(),
        P(),
        P(),
        P(),
        P(),
    )
    return jax.shard_map(
        local,
        mesh=mesh,
        in_specs=placed,
        out_specs=(P("dp", "seq", None), P("dp", "seq", None, None), P(), P(), P(), P(), P(), P()),
        check_vma=False,
    )
```

profile of v0, /device:TPU:1, one launch (start us, length us, event | category | flops | bytes accessed | tf_op | source)
XLA Modules:
  0.0 666.2 jit_solution(4487111944830111511)
XLA Ops:
  7.2 4.3 copy.31
  11.5 10.3 %all-to-all-start = ((bf16[1,16,512,128]{3,1,0,2:T(8,128)(2,1)}), bf16[1,16,512,128]{3,1,0,2:T(8,128)(2,1)S(1)}, u32[]{:S(2)}, u32[]{:S(2)}) async-start(bf16[1,16,512,128]{3,1,0,2:T(8,128)(2,1)} %copy.31), calls=%async_computation | async-start | bytes 4194304 | tf_op jit(solution)/shard_map/all_to_all | solution.py:120
  21.8 0.8 fusion.34
  22.6 2.1 collective-permute-start.1
  24.8 3.4 collective-permute-start
  28.3 16.0 %collective-permute-done.1 = bf16[1,8,1536]{2,1,0:T(8,128)(2,1)S(1)} collective-permute-done((bf16[1,8,1536]{2,1,0:T(8,128)(2,1)S(1)}, bf16[1,8,1536]{2,1,0:T(8,128)(2,1)S(1)}, u32[]{:S(2)}, u32[]{:S(2)}) %collective-permute-start.1) | collective-permute-done | bytes 24608 | tf_op jit(solution)/shard_map/ppermute | solution.py:19
  44.3 12.3 %collective-permute-done = bf16[1,8,1536]{2,1,0:T(8,128)(2,1)S(1)} collective-permute-done((bf16[1,8,1536]{2,1,0:T(8,128)(2,1)S(1)}, bf16[1,8,1536]{2,1,0:T(8,128)(2,1)S(1)}, u32[]{:S(2)}, u32[]{:S(2)}) %collective-permute-start) | collective-permute-done | bytes 24608 | tf_op jit(solution)/shard_map/ppermute | solution.py:18
  56.5 1.5 pad_maximum_fusion
  58.0 0.7 fusion.21
  59.1 51.1 %all_gather.7 = bf16[512,128]{1,0:T(8,128)(2,1)S(1)} all-gather(bf16[16,128]{1,0:T(8,128)(2,1)S(1)} %get-tuple-element.140), channel_id=1, replica_groups=mesh['dp'=8,'seq'=32] {'seq'}, dimensions={0}, use_global_device_ids=true | all-gather | bytes 135168 | tf_op jit(solution)/shard_map/all_gather | solution.py:113
  110.2 0.7 convert_element_type.161
  111.1 40.0 %all_gather.6 = bf16[512,128]{1,0:T(8,128)(2,1)S(1)} all-gather(bf16[16,128]{1,0:T(8,128)(2,1)S(1)} %get-tuple-element.142), channel_id=1, replica_groups=mesh['dp'=8,'seq'=32] {'seq'}, dimensions={0}, use_global_device_ids=true | all-gather | bytes 135168 | tf_op jit(solution)/shard_map/all_gather | solution.py:114
  151.6 1.1 copy-done.2
  152.7 1.0 fusion.20
  153.7 27.0 %while.15 = (s32[]{:T(128)}, f32[128,512]{1,0:T(8,128)S(1)}, f32[512,128]{1,0:T(8,128)}, bf16[4,2048,128]{2,1,0:T(8,128)(2,1)}, bf16[4,2048,128]{2,1,0:T(8,128)(...) while((s32[]{:T(128)}, f32[128,512]{1,0:T(8,128)S(1)}, ...), condition=%wide.region_4.5_spmd.clone, body=%wide.region_3.4_spmd.clone.sunk | while | flops 1357905920 | bytes 34472184 | solution.py:136
  153.8 0.7 fusion.78
  154.5 0.9 copy-done.8
  155.4 1.3 fusion.79
  156.7 1.7 multiply_convert_fusion.9
  158.5 0.5 convolution_add_fusion.4
  159.0 1.5 fusion.80
  160.5 0.7 fusion.78
  161.2 0.9 copy-done.8
  162.1 1.3 fusion.79
  163.5 1.7 multiply_convert_fusion.9
  165.2 0.5 convolution_add_fusion.4
  165.7 1.5 fusion.80
  167.2 0.7 fusion.78
  167.9 0.9 copy-done.8
  168.8 1.3 fusion.79
  170.2 1.7 multiply_convert_fusion.9
  171.9 0.5 convolution_add_fusion.4
  172.5 1.5 fusion.80
  174.0 0.7 fusion.78
  174.7 0.9 copy-done.8
  175.6 1.3 fusion.79
  176.9 1.7 multiply_convert_fusion.9
  178.7 0.5 convolution_add_fusion.4
  179.2 1.5 fusion.80
  180.7 4.3 copy.33
  185.0 3.8 all-to-all-start.1
  189.1 0.7 broadcast_multiply_fusion.1
  189.8 48.9 %all-to-all-done.1 = bf16[1,16,512,128]{3,1,0,2:T(8,128)(2,1)S(1)} async-done(((bf16[1,16,512,128]{3,1,0,2:T(8,128)(2,1)}), bf16[1,16,512,128]{3,1,0,2:T(8,128)(2,1)S(1)}, u32[]{:S(2)}, u32[]{:S(2)}) %all-to-all-start.1) | async-done | bytes 2097184 | tf_op jit(solution)/shard_map/all_to_all | solution.py:141
  238.7 0.5 copy.34
  239.2 0.4 convert_bitcast_fusion
  239.7 0.5 copy.35
  240.3 1.0 copy-done.3
  241.3 3.6 multiply_reduce_fusion
  244.9 0.7 broadcast_multiply_fusion
  245.9 1.2 convolution_multiply_fusion.1
  247.1 135.1 %reduce-scatter.2.cloned.1.call-done = f32[16,128]{1,0:T(8,128)} async-done(((f32[512,128]{1,0:T(8,128)}), f32[16,128]{1,0:T(8,128)}) %reduce-scatter.2.cloned.1.call-update) | async-done | bytes 8208 | tf_op jit(solution)/shard_map/reduce_scatter | solution.py:148
  382.2 1.1 multiply_reduce_fusion.2
  383.8 3.3 collective-permute-start.2
  387.1 5.8 collective-permute-start.3
  392.9 0.7 maximum_multiply_fusion
  393.6 1.2 convolution_multiply_fusion
  394.8 76.2 %psum.45 = f32[1536]{0:T(1024)} all-reduce(f32[1536]{0:T(1024)S(1)} %broadcast_multiply_fusion.2), channel_id=1, replica_groups=mesh['dp'=8,'seq'=32] {'dp','seq'}, use_global_device_ids=true, to_apply=%region_15.16 | all-reduce | flops 1536 | bytes 12288 | tf_op jit(solution)/shard_map/psum | solution.py:160
  471.2 1.0 pad_maximum_fusion.2
  472.2 182.0 %all-reduce.3.cloned.1.call-done = (f32[1536,128]{1,0:T(8,128)}, f32[1536,128]{1,0:T(8,128)}, f32[32,1536]{1,0:T(8,128)}, f32[128,512]{1,0:T(8,128)}, f32[512,128]{1,0:T(8,128)}) async-done(((f32[1536,128]{1,0:T(8,128)}, f32[1536,128]{1,0:T(8,128)}, f32[32,1536]{1,0:T(8,128)}, f32[128,512]{1,0:T(8,128)}, f32[512,128]{1,0:T(8,128)}), (f32[1536,128]{1,0:T(8,128)}, f32[1536,128]{1,0:T(8,128)}, ...) | async-done | bytes 2293776 | tf_op jit(solution)/shard_map/psum | solution.py:160
  654.2 2.2 copy.62
  656.4 0.9 copy.63
  657.2 0.7 copy.64
  657.9 0.7 copy.65
  658.6 0.7 copy.66
  (92 shorter events, 2.4 us)
Async XLA Ops:
  7.2 103.7 %copy-start = (bf16[1536,128]{1,0:T(8,128)(2,1)S(1)}, bf16[1536,128]{1,0:T(8,128)(2,1)}, u32[]{:S(2)}) copy-start(bf16[1536,128]{1,0:T(8,128)(2,1)} %param.17) | copy-start | bytes 1179652
  11.5 16.7 %copy-start.9 = (bf16[32,1536]{1,0:T(8,128)(2,1)S(1)}, bf16[32,1536]{1,0:T(8,128)(2,1)}, u32[]{:S(2)}) copy-start(bf16[32,1536]{1,0:T(8,128)(2,1)} %param.14) | copy-start | bytes 294916
  11.5 139.6 %all-to-all-start = ((bf16[1,16,512,128]{3,1,0,2:T(8,128)(2,1)}), bf16[1,16,512,128]{3,1,0,2:T(8,128)(2,1)S(1)}, u32[]{:S(2)}, u32[]{:S(2)}) async-start(bf16[1,16,512,128]{3,1,0,2:T(8,128)(2,1)} %copy.31), calls=%async_computation | async-start | bytes 4194304 | tf_op jit(solution)/shard_map/all_to_all | solution.py:120
  22.6 21.7 %collective-permute-start.1 = (bf16[1,8,1536]{2,1,0:T(8,128)(2,1)S(1)}, bf16[1,8,1536]{2,1,0:T(8,128)(2,1)S(1)}, u32[]{:S(2)}, u32[]{:S(2)}) collective-permute-start(bf16[1,8,1536]{2,1,0:T(8,128)(2,1)S(1)} %get-tuple-element.124), channel_id=1, source_target_pairs={{1,0},{2,1},{3,2},{4,3},{5,4},{6,5},{7,6},{8,7},{9,8},{10,9},{11,1... | collective-permute-start | bytes 73736 | tf_op jit(solution)/shard_map/ppermute | solution.py:19
  24.8 31.8 %collective-permute-start = (bf16[1,8,1536]{2,1,0:T(8,128)(2,1)S(1)}, bf16[1,8,1536]{2,1,0:T(8,128)(2,1)S(1)}, u32[]{:S(2)}, u32[]{:S(2)}) collective-permute-start(bf16[1,8,1536]{2,1,0:T(8,128)(2,1)S(1)} %get-tuple-element.125), channel_id=1, source_target_pairs={{0,1},{1,2},{2,3},{3,4},{4,5},{5,6},{6,7},{7,8},{8,9},{9,10},{10,1... | collective-permute-start | bytes 73736 | tf_op jit(solution)/shard_map/ppermute | solution.py:18
  28.2 30.6 %copy-start.20 = (f32[1536]{0:T(1024)S(1)}, f32[1536]{0:T(1024)}, u32[]{:S(2)}) copy-start(f32[1536]{0:T(1024)} %param.15) | copy-start | bytes 18436
  28.3 30.7 %copy-start.10 = (bf16[1536,128]{1,0:T(8,128)(2,1)S(1)}, bf16[1536,128]{1,0:T(8,128)(2,1)}, u32[]{:S(2)}) copy-start(bf16[1536,128]{1,0:T(8,128)(2,1)} %param.16) | copy-start | bytes 1179652
  58.0 93.1 %copy-start.4 = (bf16[1,256,1536]{2,1,0:T(8,128)(2,1)}, bf16[1,256,1536]{2,1,0:T(8,128)(2,1)S(1)}, u32[]{:S(2)}) copy-start(bf16[1,256,1536]{2,1,0:T(8,128)(2,1)S(1)} %get-tuple-element.122) | copy-start | bytes 2359300
  58.0 93.1 %copy-start.6 = (bf16[1,256,1536]{2,1,0:T(8,128)(2,1)}, bf16[1,256,1536]{2,1,0:T(8,128)(2,1)S(1)}, u32[]{:S(2)}) copy-start(bf16[1,256,1536]{2,1,0:T(8,128)(2,1)S(1)} %get-tuple-element.123) | copy-start | bytes 2359300
  151.1 1.6 copy-start.2
  151.2 1.6 copy-start.12
  152.7 1.0 copy-start.1
  153.8 1.6 copy-start.8
  153.8 1.6 copy-start.14
  155.4 1.4 copy-start.22
  156.7 1.7 copy-start.15
  160.5 1.6 copy-start.8
  160.5 1.6 copy-start.14
  162.1 1.4 copy-start.22
  163.4 1.7 copy-start.15
  167.2 1.6 copy-start.8
  167.2 1.6 copy-start.14
  168.8 1.4 copy-start.22
  170.2 1.7 copy-start.15
  174.0 1.6 copy-start.8
  174.0 1.6 copy-start.14
  175.6 1.4 copy-start.22
  176.9 1.7 copy-start.15
  185.0 53.7 %all-to-all-start.1 = ((bf16[1,16,512,128]{3,1,0,2:T(8,128)(2,1)}), bf16[1,16,512,128]{3,1,0,2:T(8,128)(2,1)S(1)}, u32[]{:S(2)}, u32[]{:S(2)}) async-start(bf16[1,16,512,128]{3,1,0,2:T(8,128)(2,1)} %copy.33), calls=%async_computation.1 | async-start | bytes 4194304 | tf_op jit(solution)/shard_map/all_to_all | solution.py:141
  188.8 193.3 %reduce-scatter.2.cloned.1.call-start = ((), (), s32[]{:S(2)}) async-start(), calls=%async_computation.3 | async-start | bytes 270336 | tf_op jit(solution)/shard_map/reduce_scatter | solution.py:148
  239.7 1.6 copy-start.3
  241.3 3.6 copy-start.16
  241.3 4.4 copy-start.11
  244.9 138.5 %copy-start.5 = (bf16[1,256,1536]{2,1,0:T(8,128)(2,1)S(1)}, bf16[1,256,1536]{2,1,0:T(8,128)(2,1)}, u32[]{:S(2)}) copy-start(bf16[1,256,1536]{2,1,0:T(8,128)(2,1)} %copy-done.4) | copy-start | bytes 2359300
  244.9 138.6 %copy-start.7 = (bf16[1,256,1536]{2,1,0:T(8,128)(2,1)S(1)}, bf16[1,256,1536]{2,1,0:T(8,128)(2,1)}, u32[]{:S(2)}) copy-start(bf16[1,256,1536]{2,1,0:T(8,128)(2,1)} %copy-done.6) | copy-start | bytes 2359300
  244.9 409.3 %all-reduce.3.cloned.1.call-start = ((), (), s32[]{:S(2)}) async-start(), calls=%async_computation.4 | async-start | bytes 4587520 | tf_op jit(solution)/shard_map/psum | solution.py:160
  382.2 11.4 %copy-start.21 = (f32[16,128]{1,0:T(8,128)S(1)}, f32[16,128]{1,0:T(8,128)}, u32[]{:S(2)}) copy-start(f32[16,128]{1,0:T(8,128)} %reduce-scatter.2.cloned.1.call-done) | copy-start | bytes 24580
  383.8 87.2 %collective-permute-start.2 = (bf16[1,1536]{1,0:T(2,128)(2,1)S(1)}, bf16[1,1536]{1,0:T(2,128)(2,1)S(1)}, u32[]{:S(2)}, u32[]{:S(2)}) collective-permute-start(bf16[1,1536]{1,0:T(2,128)(2,1)S(1)} %get-tuple-element.137), channel_id=1, source_target_pairs={{0,1},{1,2},{2,3},{3,4},{4,5},{5,6},{6,7},{7,8},{8,9},{9,10},{10,1... | collective-permute-start | bytes 9224 | tf_op jit(solution)/shard_map/ppermute | solution.py:18
  387.1 83.9 %collective-permute-start.3 = (bf16[1,1536]{1,0:T(2,128)(2,1)S(1)}, bf16[1,1536]{1,0:T(2,128)(2,1)S(1)}, u32[]{:S(2)}, u32[]{:S(2)}) collective-permute-start(bf16[1,1536]{1,0:T(2,128)(2,1)S(1)} %get-tuple-element.138), channel_id=1, source_target_pairs={{1,0},{2,1},{3,2},{4,3},{5,4},{6,5},{7,6},{8,7},{9,8},{10,9},{11,1... | collective-permute-start | bytes 9224 | tf_op jit(solution)/shard_map/ppermute | solution.py:19
  654.2 2.2 copy-start.13
  654.2 3.1 copy-start.19
  654.2 3.7 copy-start.18
  654.2 4.4 copy-start.17
Sparse Core Ops, SparseCore 0:
  245.0 137.1 reduce-scatter.1
  394.9 259.1 all-reduce.2
where the time goes:
time: 667 us; the launch traced here: 666 us
  waiting for transfers between devices  394 us (59%)
  blocking collectives  167 us (25%)
  starting transfers between devices  29.1 us (4%)
  matrix products  27.1 us (4%)
  local copies, waits for them, and re-layouts  22 us (3%)
  between operations  14.4 us (2%)
  other arithmetic  11.8 us (2%)
    psum x1, waiting for transfers between devices, local(): lax.psum((contract_rows(normed, grad_left) * grad_scale, contract_rows(no...  182 us
    reduce_scatter x1, waiting for transfers between devices, local(): lax.psum_scatter(partial_right, 'seq', scatter_dimension=0, tiled=True)  135 us
    psum x1, blocking collectives, local(): lax.psum((contract_rows(normed, grad_left) * grad_scale, contract_rows(no...  76.2 us
    all_gather x1, blocking collectives, local(): lax.all_gather(left_proj, 'seq', axis=0, tiled=True)  51.1 us
    all_to_all x1, waiting for transfers between devices, local(): lax.all_to_all(grad_sym[None], 'seq', split_axis=2, concat_axis=1, tiled=...  48.9 us
    all_gather x1, blocking collectives, local(): lax.all_gather(right_proj, 'seq', axis=0, tiled=True)  40 us
    ppermute x2, waiting for transfers between devices, extended_2(): after = lax.ppermute(leading, axis, down)  16 us
  transfers between devices with their start and end apart: 8, of which 5 were waited for; matrix products, arithmetic and copies ran while one was open for 2% of the time, Pallas kernels for 0%

commit v1 on v0

v1 whole, which is shorter than its diff:
```python
import functools
import math

import jax
import jax.numpy as jnp
from jax import lax
from jax.experimental import pallas as pl
from jax.experimental.pallas import tpu as pltpu
from jax.sharding import PartitionSpec as P

POOL = 16
NB = 12
F32 = jnp.float32
BF16 = jnp.bfloat16
MESH = pl.DeviceIdType.MESH


def dot(a, b, ca, cb):
    return lax.dot_general(a, b, (((ca,), (cb,)), ((), ())), preferred_element_type=F32)


def body(
    scale,
    tokens,
    pair,
    cot,
    taps,
    gain,
    lw,
    rw,
    wa,
    wb,
    g_tokens,
    g_pair,
    g_lw,
    g_rw,
    g_taps,
    g_gain,
    g_wa,
    g_wb,
    tokv,
    gtokv,
    pairv,
    cotv,
    recv,
    obuf,
    rbuf,
    feats,
    perm,
    wcat,
    cen,
    up,
    dn,
    normed,
    gpx,
    halo_out,
    halo_in,
    accl,
    accr,
    wacc,
    acc,
    send_a,
    recv_a,
    send_b,
    recv_b,
    mid,
    recv_c,
    fin,
    gat,
    loc,
    osem,
    tile_s,
    tile_r,
    feat_s,
    feat_r,
    ret_s,
    ret_r,
    halo_s,
    halo_r,
    a_s,
    a_r,
    b_s,
    b_r,
    c_s,
    c_r,
    f_s,
    f_r,
    d_s,
    d_r,
    e_s,
    e_r,
):
    dpi = lax.axis_index("dp")
    me = lax.axis_index("seq")
    x, zh = lax.div(dpi, 2), lax.rem(dpi, 2)
    chip, core = lax.div(me, 2), lax.rem(me, 2)
    y, zl = lax.div(chip, 4), lax.rem(chip, 4)
    zz = zh * 4 + zl
    partner = chip * 2 + 1 - core

    def step(s):
        late = s >= 12
        dy = jnp.where(late, s - 11, lax.div(s, 3))
        dz = jnp.where(late, 0, 1 + lax.rem(s + 1, 3))
        return dy, dz

    def target(s):
        dy, dz = step(s)
        q = lax.rem(y + dy, 4) * 4 + lax.rem(zl + dz, 4)
        return q * 2 + jnp.where(q > chip, core, 1 - core)

    def source(s):
        dy, dz = step(s)
        r = lax.rem(y + 4 - dy, 4) * 4 + lax.rem(zl + 4 - dz, 4)
        return r * 2 + jnp.where(r < chip, core, 1 - core)

    def in_seq(k):
        return (dpi, k)

    def plane(u):
        px, py = lax.rem(x + lax.div(u, 4), 4), lax.rem(y + lax.rem(u, 4), 4)
        return px * 4 + py, (px * 2 + zh, py * 8 + zl * 2 + core)

    def ring(v):
        t = lax.rem(zz + v, 8)
        return t, (x * 2 + lax.div(t, 4), y * 8 + lax.rem(t, 4) * 2 + core)

    def remote(src, dst, ssem, rsem, dev):
        return pltpu.make_async_remote_copy(
            src_ref=src, dst_ref=dst, send_sem=ssem, recv_sem=rsem, device_id=dev, device_id_type=MESH
        )

    def cols(k):
        return pl.ds(pl.multiple_of(k * 16, 16), 16)

    def loop(lo, hi, f):
        def g(i, carry):
            f(i)
            return carry

        lax.fori_loop(lo, hi, g, 0)

    local = [
        pltpu.make_async_copy(tokens, tokv, loc.at[0]),
        pltpu.make_async_copy(lw, wcat.at[:, pl.ds(0, 128)], loc.at[1]),
        pltpu.make_async_copy(rw, wcat.at[:, pl.ds(128, 128)], loc.at[2]),
        pltpu.make_async_copy(pair, pairv, loc.at[3]),
        pltpu.make_async_copy(cot, cotv, loc.at[4]),
        pltpu.make_async_copy(pair.at[:, cols(me), :], recv.at[16, 0], loc.at[5]),
        pltpu.make_async_copy(cot.at[:, cols(me), :], recv.at[16, 1], loc.at[6]),
    ]
    for c in local:
        c.start()

    barrier = pltpu.get_barrier_semaphore()

    def greet(dev):
        pl.semaphore_signal(barrier, inc=1, device_id=dev, device_id_type=MESH)

    def greet_seq(s):
        greet(in_seq(target(s)))
        greet(in_seq(source(s)))

    loop(0, 15, greet_seq)
    greet(in_seq(partner))
    loop(4, 16, lambda u: greet(plane(u)[1]))
    loop(0, 4, lambda v: greet((x * 2 + 1 - zh, y * 8 + v * 2 + core)))
    pl.semaphore_wait(barrier, 47)

    def tile_copy(s, k, dev):
        return remote(
            (pair, cot)[k].at[:, cols(dev), :], recv.at[s, k], tile_s.at[s, k], tile_r.at[s, k], in_seq(dev)
        )

    def send_tile(s):
        dev = target(s)
        tile_copy(s, 0, dev).start()
        tile_copy(s, 1, dev).start()

    loop(0, 15, send_tile)
    tile_copy(15, 0, partner).start()
    tile_copy(15, 1, partner).start()

    row = lax.broadcasted_iota(jnp.int32, (256, 256), 0)
    col = lax.broadcasted_iota(jnp.int32, (256, 256), 1)
    perm[...] = jnp.where(col == (row & 15) * 16 + (row >> 4), 1.0, 0.0).astype(BF16)
    wacc[...] = jnp.zeros_like(wacc)
    accl[...] = jnp.zeros_like(accl)
    accr[...] = jnp.zeros_like(accr)

    def lanes(b):
        return pl.ds(pl.multiple_of(b * 128, 128), 128)

    local[0].wait()

    def tap_parts(b):
        k = taps[:, lanes(b)].astype(F32)
        return k[0:8], k[8:16], k[16:24], k[24:32]

    def pool(b):
        k0, k1, k2, k3 = tap_parts(b)
        for p in range(16):
            t = tokv[p * 16 : p * 16 + 16, lanes(b)].astype(F32)
            lo, hi = t[0:8], t[8:16]
            cen[b, p : p + 1] = jnp.sum(lo * k1 + hi * k2, axis=0, keepdims=True)
            up[b, p + 1 : p + 2] = jnp.sum(hi * k0, axis=0, keepdims=True)
            dn[b, p : p + 1] = jnp.sum(lo * k3, axis=0, keepdims=True)
        halo_out[0, b] = dn[b, 0:1]
        halo_out[1, b] = up[b, 16:17]

    loop(0, NB, pool)
    left, right = lax.rem(me + 31, 32), lax.rem(me + 1, 32)

    def halo(k, j, dev):
        return remote(halo_out.at[k], halo_in.at[k], halo_s.at[k], halo_r.at[k], in_seq(dev))

    def halo_pair(k):
        return halo(k, 0, left), halo(k + 1, 1, right)

    to_left, to_right = halo_pair(0)
    to_left.start()
    to_right.start()
    to_left.wait()
    to_right.wait()
    first = jnp.where(me == 0, 0.0, 1.0)
    last = jnp.where(me == 31, 0.0, 1.0)

    def finish_pool(b, total):
        up[b, 0:1] = halo_in[1, b] * first
        dn[b, 16:17] = halo_in[0, b] * last
        v = cen[b] + up[b, 0:16] + dn[b, 1:17]
        cen[b] = v
        return total + v * v

    squares = lax.fori_loop(0, NB, finish_pool, jnp.zeros((16, 128), F32))
    inv = lax.rsqrt(jnp.sum(squares, axis=1, keepdims=True) / (NB * 128.0) + 1e-6)
    local[1].wait()
    local[2].wait()

    def project(b, total):
        n = (cen[b] * inv * gain[b]).astype(BF16)
        normed[b] = n
        return total + dot(n, wcat[pl.ds(pl.multiple_of(b * 128, 128), 128), :], 1, 0)

    feats[me] = lax.fori_loop(0, NB, project, jnp.zeros((16, 256), F32)).astype(BF16)

    def feat_copy(slot, dev):
        return remote(feats.at[me], feats.at[me], feat_s.at[slot], feat_r.at[me], in_seq(dev))

    def feat_arrived(k):
        remote(feats.at[k], feats.at[k], feat_s.at[31], feat_r.at[k], in_seq(k)).wait_recv()

    def send_feat(s):
        feat_copy(s, source(s)).start()
        feat_copy(15 + s, target(s)).start()

    feat_copy(30, partner).start()
    loop(0, 15, send_feat)

    for c in local[3:]:
        c.wait()

    def out_copy(slot, k):
        return pltpu.make_async_copy(obuf.at[slot], g_pair.at[:, cols(k), :], osem.at[slot])

    def add_left_right(grad, f):
        accl[...] += grad * f[:, 128:][None]
        accr[...] += grad * f[:, :128][None]

    def tile(s, k, weight):
        own = jnp.concatenate(
            [pairv[:, cols(k), :].reshape(256, 128), cotv[:, cols(k), :].reshape(256, 128)], axis=1
        )
        other = jnp.concatenate([recv[s, 0].reshape(256, 128), recv[s, 1].reshape(256, 128)], axis=1)
        both = own.astype(F32) + dot(perm[...], other, 1, 0)
        mine, theirs = feats[me].astype(F32), feats[k].astype(F32)
        outer = mine[:, None, :128] * theirs[None, :, 128:] + mine[:, None, 128:] * theirs[None, :, :128]
        sym = (both[:, :128] + outer.reshape(256, 128)).astype(BF16)
        cs = both[:, 128:]
        csb = cs.astype(BF16)
        pre = dot(sym, wa[...], 1, 0)
        sig = 0.5 * jnp.tanh(0.5 * pre) + 0.5
        act = pre * sig
        gpre = (dot(csb, wb[...], 1, 1) * (sig + act * (1.0 - sig))).astype(BF16)
        grad = cs + dot(gpre, wa[...], 1, 1)
        wacc[0] += dot(sym, gpre, 0, 0) * weight
        wacc[1] += dot(csb, act.astype(BF16), 0, 0) * weight
        add_left_right(grad.reshape(16, 16, 128), theirs)
        gradb = grad.astype(BF16)
        obuf[s] = gradb.reshape(16, 16, 128)
        out_copy(s, k).start()
        return gradb

    tile(16, me, 0.5)
    tile_copy(15, 0, partner).wait()
    tile_copy(15, 1, partner).wait()
    feat_arrived(partner)
    tile(15, partner, 0.5)

    def ret_copy(s, dev):
        return remote(rbuf.at[s], obuf.at[17 + s], ret_s.at[s], ret_r.at[s], in_seq(dev))

    def owned(s):
        k = source(s)
        dev = target(s)
        feat_arrived(k)
        tile_copy(s, 0, dev).wait_recv()
        tile_copy(s, 1, dev).wait_recv()
        gradb = tile(s, k, 1.0)
        rbuf[s] = dot(perm[...], gradb, 1, 0).astype(BF16).reshape(16, 16, 128)
        ret_copy(s, k).start()

    loop(0, 15, owned)

    def returned(s):
        k = target(s)
        feat_arrived(k)
        ret_copy(s, source(s)).wait_recv()
        out_copy(17 + s, k).start()
        add_left_right(obuf[17 + s].astype(F32), feats[k].astype(F32))

    loop(0, 15, returned)

    glr = jnp.concatenate(
        [jnp.sum(accl[...], axis=1).astype(BF16), jnp.sum(accr[...], axis=1).astype(BF16)], axis=1
    )

    def grad_norm(b, carry):
        total, unused = carry
        gn = dot(glr, wcat[pl.ds(pl.multiple_of(b * 128, 128), 128), :], 1, 1)
        scaled = gn * gain[b]
        gpx[b, 1:17] = scaled
        acc[24, 8, pl.ds(b, 1)] = jnp.sum(gn * cen[b] * inv, axis=0, keepdims=True) * scale
        return total + scaled * cen[b], unused

    for g in range(24, 32):
        acc[g, 8] = jnp.zeros((16, 128), F32)
    total, _ = lax.fori_loop(0, NB, grad_norm, (jnp.zeros((16, 128), F32), 0))
    mean = jnp.sum(total, axis=1, keepdims=True) / (NB * 128.0) * inv * inv * inv

    def grad_pool(b):
        v = (gpx[b, 1:17] * inv - cen[b] * mean).astype(BF16).astype(F32)
        gpx[b, 1:17] = v
        halo_out[2, b] = v[0:1]
        halo_out[3, b] = v[15:16]

    loop(0, NB, grad_pool)
    to_left2, to_right2 = halo_pair(2)
    to_left2.start()
    to_right2.start()

    def features_grad(b):
        prod = dot(normed[b], glr, 0, 0) * scale
        acc[b, 0:8] = prod[:, :128].reshape(8, 16, 128)
        acc[b + 12, 0:8] = prod[:, 128:].reshape(8, 16, 128)

    loop(0, NB, features_grad)
    for q in range(4):
        lane = slice(q * 128, q * 128 + 128)
        acc[24 + q, 0:8] = (wacc[0, :, lane] * scale).reshape(8, 16, 128)
        acc[28 + q, 0:8] = (wacc[1, :, lane].T * scale).reshape(8, 16, 128)

    to_left2.wait()
    to_right2.wait()

    def token_grad(b):
        k0, k1, k2, k3 = tap_parts(b)
        gpx[b, 0:1] = halo_in[3, b] * first
        gpx[b, 17:18] = halo_in[2, b] * last
        s0 = s1 = s2 = s3 = jnp.zeros((8, 128), F32)
        for p in range(16):
            before, here, after = gpx[b, p : p + 1], gpx[b, p + 1 : p + 2], gpx[b, p + 2 : p + 3]
            t = tokv[p * 16 : p * 16 + 16, lanes(b)].astype(F32)
            lo, hi = t[0:8], t[8:16]
            s0 = s0 + after * hi
            s1 = s1 + here * lo
            s2 = s2 + here * hi
            s3 = s3 + before * lo
            g = jnp.concatenate([here * k1 + before * k3, here * k2 + after * k0], axis=0)
            gtokv[p * 16 : p * 16 + 16, lanes(b)] = g.astype(BF16)
        acc[2 * b, 8, 0:8] = s0 * scale
        acc[2 * b, 8, 8:16] = s1 * scale
        acc[2 * b + 1, 8, 0:8] = s2 * scale
        acc[2 * b + 1, 8, 8:16] = s3 * scale

    loop(0, NB, token_grad)
    tok_out = pltpu.make_async_copy(gtokv, g_tokens, loc.at[7])
    tok_out.start()

    def a_copy(j):
        return remote(send_a.at[j], recv_a.at[j], a_s.at[j], a_r.at[j], in_seq(partner))

    def to_partner(u):
        j = plane(u)[0]
        send_a[j] = acc[(1 - core) * 16 + j].astype(BF16)
        a_copy(j).start()

    loop(0, 16, to_partner)

    def b_copy(u, dev):
        return remote(send_b.at[u], recv_b.at[u], b_s.at[u], b_r.at[u], dev)

    jme = x * 4 + y
    a_copy(jme).wait_recv()
    mid[...] = acc[core * 16 + jme] + recv_a[jme].astype(F32)

    def to_plane(u):
        j, dev = plane(u)
        a_copy(j).wait_recv()
        send_b[u] = (acc[core * 16 + j] + recv_a[j].astype(F32)).astype(BF16)
        b_copy(u, dev).start()

    loop(1, 16, to_plane)

    def from_plane(u):
        b_copy(u, plane(u)[1]).wait_recv()
        mid[...] += recv_b[u].astype(F32)

    loop(1, 16, from_plane)

    def c_copy(t, dev, slot):
        return (
            remote(mid.at[t], recv_c.at[slot, 0], c_s.at[t, 0], c_r.at[slot, 0], dev),
            remote(mid.at[8], recv_c.at[slot, 1], c_s.at[t, 1], c_r.at[slot, 1], dev),
        )

    def to_ring(v):
        t, dev = ring(v)
        for c in c_copy(t, dev, zz):
            c.start()

    loop(1, 8, to_ring)
    recv_c[zz, 0] = mid[zz]
    recv_c[zz, 1] = mid[8]

    def from_ring(v):
        t, dev = ring(v)
        for c in c_copy(t, dev, t):
            c.wait_recv()

    loop(1, 8, from_ring)
    summed = recv_c[0]
    for t in range(1, 8):
        summed = summed + recv_c[t]
    fin[zz] = summed[0].astype(BF16)
    fin[8] = summed[1].astype(BF16)

    def f_copy(slot, v, dev):
        return remote(fin.at[slot], fin.at[slot], f_s.at[v], f_r.at[slot], dev)

    loop(1, 8, lambda v: f_copy(zz, v, ring(v)[1]).start())
    loop(1, 8, lambda v: f_copy(ring(v)[0], v, ring(v)[1]).wait_recv())

    def d_copy(u, dev, j):
        return remote(fin, gat.at[core * 16 + j], d_s.at[u], d_r.at[j], dev)

    loop(1, 16, lambda u: d_copy(u, plane(u)[1], jme).start())
    gat[core * 16 + jme] = fin[...]

    def e_copy(j, half):
        slot = gat.at[half * 16 + j]
        return remote(slot, slot, e_s.at[j], e_r.at[j], in_seq(partner))

    e_copy(jme, core).start()

    def forward(u):
        j, dev = plane(u)
        d_copy(u, dev, j).wait_recv()
        e_copy(j, core).start()

    loop(1, 16, forward)
    loop(0, 16, lambda j: e_copy(j, 1 - core).wait_recv())

    for b in range(NB):
        rows = slice(b * 128, b * 128 + 128)
        g_lw[rows, :] = gat[b, 0:8].reshape(128, 128).astype(F32)
        g_rw[rows, :] = gat[b + 12, 0:8].reshape(128, 128).astype(F32)
        g_taps[0:16, rows] = gat[2 * b, 8].astype(F32)
        g_taps[16:32, rows] = gat[2 * b + 1, 8].astype(F32)
    gains = gat[24, 8].astype(F32)
    for b in range(NB):
        g_gain[:, b * 128 : b * 128 + 128] = gains[b : b + 1]
    for q in range(4):
        lane = slice(q * 128, q * 128 + 128)
        g_wa[:, lane] = gat[24 + q, 0:8].reshape(128, 128).astype(F32)
        g_wb[lane, :] = gat[28 + q, 0:8].reshape(128, 128).astype(F32)

    def drain_tile(s):
        dev = target(s)
        tile_copy(s, 0, dev).wait_send()
        tile_copy(s, 1, dev).wait_send()
        feat_copy(s, source(s)).wait_send()
        feat_copy(15 + s, dev).wait_send()
        ret_copy(s, source(s)).wait_send()
        out_copy(17 + s, dev).wait()

    loop(0, 15, drain_tile)
    feat_copy(30, partner).wait_send()
    loop(0, 17, lambda s: out_copy(s, me).wait())
    tok_out.wait()

    def drain_sum(u):
        j, dev = plane(u)
        b_copy(u, dev).wait_send()
        d_copy(u, dev, j).wait_send()

    loop(1, 16, drain_sum)
    loop(0, 16, lambda j: a_copy(j).wait_send())
    loop(0, 16, lambda j: e_copy(j, core).wait_send())

    def drain_ring(v):
        t, dev = ring(v)
        for c in c_copy(t, dev, zz):
            c.wait_send()
        f_copy(zz, v, dev).wait_send()

    loop(1, 8, drain_ring)


def local(tokens, pair_in, cotangent, kernel, norm_gain, left_weight, right_weight, transition_a, transition_b):
    plen = pair_in.shape[2]
    scale = 1.0 / math.sqrt(lax.axis_size("dp") * plen * plen)
    vmem = pl.BlockSpec(memory_space=pltpu.VMEM)
    hbm = pl.BlockSpec(memory_space=pl.ANY)
    dma = pltpu.SemaphoreType.DMA
    tile = (16, 16, 128)
    chunk = (9, 16, 128)
    outs = pl.pallas_call(
        functools.partial(body, scale),
        out_shape=(
            jax.ShapeDtypeStruct((256, 1536), BF16),
            jax.ShapeDtypeStruct((16, 512, 128), BF16),
            jax.ShapeDtypeStruct((1536, 128), F32),
            jax.ShapeDtypeStruct((1536, 128), F32),
            jax.ShapeDtypeStruct((32, 1536), F32),
            jax.ShapeDtypeStruct((1, 1536), F32),
            jax.ShapeDtypeStruct((128, 512), F32),
            jax.ShapeDtypeStruct((512, 128), F32),
        ),
        in_specs=[hbm, hbm, hbm, vmem, vmem, hbm, hbm, vmem, vmem],
        out_specs=(hbm, hbm) + (vmem,) * 6,
        scratch_shapes=[
            pltpu.VMEM((256, 1536), BF16),
            pltpu.VMEM((256, 1536), BF16),
            pltpu.VMEM((16, 512, 128), BF16),
            pltpu.VMEM((16, 512, 128), BF16),
            pltpu.VMEM((17, 2) + tile, BF16),
            pltpu.VMEM((32,) + tile, BF16),
            pltpu.VMEM((15,) + tile, BF16),
            pltpu.VMEM((32, 16, 256), BF16),
            pltpu.VMEM((256, 256), BF16),
            pltpu.VMEM((1536, 256), BF16),
            pltpu.VMEM((NB, 16, 128), F32),
            pltpu.VMEM((NB, 24, 128), F32),
            pltpu.VMEM((NB, 24, 128), F32),
            pltpu.VMEM((NB, 16, 128), BF16),
            pltpu.VMEM((NB, 24, 128), F32),
            pltpu.VMEM((4, NB, 1, 128), F32),
            pltpu.VMEM((4, NB, 1, 128), F32),
            pltpu.VMEM(tile, F32),
            pltpu.VMEM(tile, F32),
            pltpu.VMEM((2, 128, 512), F32),
            pltpu.VMEM((32,) + chunk, F32),
            pltpu.VMEM((16,) + chunk, BF16),
            pltpu.VMEM((16,) + chunk, BF16),
            pltpu.VMEM((16,) + chunk, BF16),
            pltpu.VMEM((16,) + chunk, BF16),
            pltpu.VMEM(chunk, F32),
            pltpu.VMEM((8, 2, 16, 128), F32),
            pltpu.VMEM(chunk, BF16),
            pltpu.VMEM((32,) + chunk, BF16),
            dma((8,)),
            dma((32,)),
            dma((16, 2)),
            dma((16, 2)),
            dma((32,)),
            dma((32,)),
            dma((15,)),
            dma((15,)),
            dma((4,)),
            dma((4,)),
            dma((16,)),
            dma((16,)),
            dma((16,)),
            dma((16,)),
            dma((8, 2)),
            dma((8, 2)),
            dma((8,)),
            dma((8,)),
            dma((16,)),
            dma((16,)),
            dma((16,)),
            dma((16,)),
        ],
        compiler_params=pltpu.CompilerParams(
            collective_id=0, has_side_effects=True, vmem_limit_bytes=48 * 1024 * 1024
        ),
    )(
        tokens[0],
        pair_in[0],
        cotangent[0],
        kernel,
        norm_gain.reshape(NB, 1, 128),
        left_weight,
        right_weight,
        transition_a,
        transition_b,
    )
    return (outs[0][None], outs[1][None], outs[2], outs[3], outs[4], outs[5].reshape(1536), outs[6], outs[7])


def solution(mesh):
    placed = (
        P("dp", "seq", None),
        P("dp", "seq", None, None),
        P("dp", "seq", None, None),
        P(),
        P(),
        P(),
        P(),
        P(),
        P(),
    )
    return jax.shard_map(
        local,
        mesh=mesh,
        in_specs=placed,
        out_specs=(P("dp", "seq", None), P("dp", "seq", None, None), P(), P(), P(), P(), P(), P()),
        check_vma=False,
    )
```

time: 667 us -> 149 us (0.22)
  waiting for transfers between devices: 394 us -> 0 us
  blocking collectives: 167 us -> 0 us
  Pallas kernels: 0 us -> 133 us
  starting transfers between devices: 29.1 us -> 0 us
  matrix products: 27.1 us -> 0 us
  between operations: 14.4 us -> 0.65 us
  other arithmetic: 11.8 us -> 0.62 us
  local copies, waits for them, and re-layouts: 22 us -> 14.4 us
    psum x1 -> x0, waiting for transfers between devices: 182 us -> none  [local(): lax.psum((contract_rows(normed, grad_left) * grad_scale, contract_rows(no...]
    reduce_scatter x1 -> x0, waiting for transfers between devices: 135 us -> none  [local(): lax.psum_scatter(partial_right, 'seq', scatter_dimension=0, tiled=True)]
    pallas_call x0 -> x1, Pallas kernels: none -> 133 us  [local(): pl.pallas_call(functools.partial(body, scale), out_shape=(jax.ShapeDtypeS...]
    all_gather x2 -> x0, blocking collectives: 91.1 us -> none  [the longest x1 51.1 us: local(): lax.all_gather(left_proj, 'seq', axis=0, tiled=True)]
    psum x1 -> x0, blocking collectives: 76.2 us -> none  [local(): lax.psum((contract_rows(normed, grad_left) * grad_scale, contract_rows(no...]
    all_to_all x2 -> x0, waiting for transfers between devices: 48.9 us -> none  [the longest x1 48.9 us: local(): lax.all_to_all(grad_sym[None], 'seq', split_axis=2, concat_axis=1, tiled=...]
    ppermute x4 -> x0, waiting for transfers between devices: 28.3 us -> none  [the longest x2 16 us: extended_2(): after = lax.ppermute(leading, axis, down)]
    dot_general x26 -> x0, matrix products: 27.1 us -> none  [the longest x10 9.77 us: contract_rows(): lax.dot_general(first_arr, second_arr, (((0,), (0,)), ((), ())), preferre...]
  transfers between devices with their start and end apart: 8 -> 0, of which waited for: 5 -> 0; matrix products, arithmetic and copies ran while one was open for 2% -> 0% of each run, Pallas kernels for 0% -> 0%
where the time goes in v1:
time: 149 us
  Pallas kernels  133 us (89%)
  local copies, waits for them, and re-layouts  14.4 us (10%)
    pallas_call x1, Pallas kernels, local(): pl.pallas_call(functools.partial(body, scale), out_shape=(jax.ShapeDtypeS...  133 us
    unnamed x19, local copies, waits for them, and re-layouts  13.7 us

profile of v1, /device:TPU:1, one launch (start us, length us, event | category | flops | bytes accessed | tf_op | source)
XLA Modules:
  0.0 148.6 jit_solution(18057547610316152693)
XLA Ops:
  0.6 0.7 reshape.22.gain
  1.3 0.0 copy-start
  1.3 1.1 copy-done
  2.5 0.0 copy-start.1
  2.5 1.0 copy-done.1
  3.5 0.0 copy-start.2
  3.5 1.0 copy-done.2
  4.5 0.0 copy-start.3
  4.5 0.9 copy-done.3
  5.4 0.0 copy-start.4
  5.4 0.9 copy-done.4
  6.3 0.0 copy-start.5
  6.3 0.9 copy-done.5
  7.2 132.9 %shard_map.152 = (bf16[256,1536]{1,0:T(8,128)(2,1)S(1)}, bf16[16,512,128]{2,1,0:T(8,128)(2,1)}, f32[1536,128]{1,0:T(8,128)S(1)}, f32[1536,128]{1,0:T(8,128)S(1)}...) custom-call(bf16[256,1536]{1,0:T(8,128)(2,1)S(1)} %bitcast.5, ...), custom_call_target="tpu_custom_call" | custom-call | tf_op jit(solution)/shard_map/pallas_call | solution.py:528
  140.1 0.6 reduce
  140.7 0.9 copy.24
  141.6 3.1 %copy.25 = bf16[1,16,512,128]{3,2,1,0:T(8,128)(2,1)} copy(bf16[1,16,512,128]{3,2,1,0:T(8,128)(2,1)} %bitcast.9) | data formatting | bytes 4194304
  144.7 0.9 copy.26
  145.6 0.9 copy.27
  146.5 0.7 copy.28
  147.2 0.7 copy.29
  147.9 0.7 copy.30
Async XLA Ops:
  1.3 1.1 copy-start
  2.5 1.0 copy-start.1
  3.5 1.0 copy-start.2
  4.5 0.9 copy-start.3
  5.4 0.9 copy-start.4
  6.3 0.9 copy-start.5

commit v2 on v1

v2 whole, which is shorter than its diff:
```python
import functools
import math

import jax
import jax.numpy as jnp
from jax import lax
from jax.experimental import pallas as pl
from jax.experimental.pallas import tpu as pltpu
from jax.sharding import PartitionSpec as P

POOL = 16
NB = 12
EARLY = 2
VMEM_LIMIT = 58 * 1024 * 1024
F32 = jnp.float32
BF16 = jnp.bfloat16
MESH = pl.DeviceIdType.MESH


def dot(a, b, ca, cb):
    return lax.dot_general(a, b, (((ca,), (cb,)), ((), ())), preferred_element_type=F32)


def body(
    scale,
    tokens,
    pair,
    cot,
    taps_h,
    gain_h,
    lw,
    rw,
    wa_h,
    wb_h,
    g_tokens,
    g_pair,
    gat,
    gtokv,
    gpair,
    tokv,
    tokh,
    pairv,
    cotv,
    recv,
    rbuf,
    feats,
    perm,
    wcat,
    taps,
    gain,
    wa,
    wb,
    cen,
    up,
    dn,
    normed,
    gpx,
    halo_out,
    halo_in,
    accl,
    accr,
    wacc,
    glr_out,
    nin,
    gin,
    w3_out,
    w3_in,
    w2_out,
    w2_in,
    mid,
    recv_c,
    fin,
    loc,
    tile_s,
    tile_r,
    feat_s,
    feat_r,
    ret_s,
    ret_r,
    halo_s,
    halo_r,
    th_s,
    th_r,
    n_s,
    n_r,
    g_s,
    g_r,
    w3_s,
    w3_r,
    w2_s,
    w2_r,
    c_s,
    c_r,
    f_s,
    f_r,
    d_s,
    d_r,
    e_s,
    e_r,
):
    dpi = lax.axis_index("dp")
    me = lax.axis_index("seq")
    x, zh = lax.div(dpi, 2), lax.rem(dpi, 2)
    chip, core = lax.div(me, 2), lax.rem(me, 2)
    y, zl = lax.div(chip, 4), lax.rem(chip, 4)
    zz = zh * 4 + zl
    partner = chip * 2 + 1 - core

    def step(s):
        late = s >= 12
        dy = jnp.where(late, s - 11, lax.div(s, 3))
        dz = jnp.where(late, 0, 1 + lax.rem(s + 1, 3))
        return dy, dz

    def target(s):
        dy, dz = step(s)
        q = lax.rem(y + dy, 4) * 4 + lax.rem(zl + dz, 4)
        return q * 2 + jnp.where(q > chip, core, 1 - core)

    def source(s):
        dy, dz = step(s)
        r = lax.rem(y + 4 - dy, 4) * 4 + lax.rem(zl + 4 - dz, 4)
        return r * 2 + jnp.where(r < chip, core, 1 - core)

    def in_seq(k):
        return (dpi, k)

    def plane(u):
        px, py = lax.rem(x + lax.div(u, 4), 4), lax.rem(y + lax.rem(u, 4), 4)
        return chunk_of(px, py, core), (px * 2 + zh, py * 8 + zl * 2 + core)

    def chunk_of(px, py, pc):
        odd = lax.rem(px + py, 2)
        return jnp.where(pc == 0, px * 4 + py, 16 + (1 - odd) * 8 + px * 2 + lax.div(py, 2))

    def owner(g):
        t = lax.rem(g, 16)
        e, r = lax.div(t, 8), lax.rem(t, 8)
        rx = lax.div(r, 2)
        ry = lax.rem(r, 2) * 2 + lax.rem(1 - e + rx, 2)
        px = jnp.where(g < 16, lax.div(t, 4), rx)
        py = jnp.where(g < 16, lax.rem(t, 4), ry)
        return (px * 2 + zh, py * 8 + zl * 2 + lax.div(g, 16))

    mine = chunk_of(x, y, core)

    def ring(v):
        t = lax.rem(zz + v, 8)
        return t, (x * 2 + lax.div(t, 4), y * 8 + lax.rem(t, 4) * 2 + core)

    def remote(src, dst, ssem, rsem, dev):
        return pltpu.make_async_remote_copy(
            src_ref=src, dst_ref=dst, send_sem=ssem, recv_sem=rsem, device_id=dev, device_id_type=MESH
        )

    def cols(k):
        return pl.ds(pl.multiple_of(k * 16, 16), 16)

    def loop(lo, hi, f):
        def g(i, carry):
            f(i)
            return carry

        lax.fori_loop(lo, hi, g, 0)

    local = [
        pltpu.make_async_copy(tokens, tokv, loc.at[0]),
        pltpu.make_async_copy(taps_h, taps, loc.at[1]),
        pltpu.make_async_copy(gain_h, gain, loc.at[2]),
        pltpu.make_async_copy(lw, wcat.at[:, pl.ds(0, 128)], loc.at[3]),
        pltpu.make_async_copy(rw, wcat.at[:, pl.ds(128, 128)], loc.at[4]),
        pltpu.make_async_copy(wa_h, wa, loc.at[5]),
        pltpu.make_async_copy(wb_h, wb, loc.at[6]),
        pltpu.make_async_copy(pair, pairv, loc.at[7]),
        pltpu.make_async_copy(cot, cotv, loc.at[8]),
        pltpu.make_async_copy(pair.at[:, cols(me), :], recv.at[16, 0], loc.at[9]),
        pltpu.make_async_copy(cot.at[:, cols(me), :], recv.at[16, 1], loc.at[10]),
    ]
    for c in local:
        c.start()

    barrier = pltpu.get_barrier_semaphore()

    def greet(dev):
        pl.semaphore_signal(barrier, inc=1, device_id=dev, device_id_type=MESH)

    def greet_seq(s):
        greet(in_seq(target(s)))
        greet(in_seq(source(s)))

    loop(0, 15, greet_seq)
    greet(in_seq(partner))
    def greet_plane(u):
        px, py = lax.rem(x + lax.div(u, 4), 4), lax.rem(y + lax.rem(u, 4), 4)
        greet((px * 2 + zh, py * 8 + zl * 2 + core))
        greet((px * 2 + zh, py * 8 + zl * 2 + 1 - core))

    loop(4, 16, greet_plane)
    loop(0, 4, lambda v: greet((x * 2 + 1 - zh, y * 8 + v * 2 + core)))

    def tile_copy(s, k, dev):
        return remote(
            (pair, cot)[k].at[:, cols(dev), :], recv.at[s, k], tile_s.at[s, k], tile_r.at[s, k], in_seq(dev)
        )

    def send_tile(s):
        dev = target(s)
        tile_copy(s, 0, dev).start()
        tile_copy(s, 1, dev).start()

    row = lax.broadcasted_iota(jnp.int32, (256, 256), 0)
    col = lax.broadcasted_iota(jnp.int32, (256, 256), 1)
    perm[...] = jnp.where(col == (row & 15) * 16 + (row >> 4), 1.0, 0.0).astype(BF16)
    wacc[...] = jnp.zeros_like(wacc)
    accl[...] = jnp.zeros_like(accl)
    accr[...] = jnp.zeros_like(accr)

    def lanes(b):
        return pl.ds(pl.multiple_of(b * 128, 128), 128)

    local[0].wait()
    local[1].wait()

    def tap_parts(b):
        k = taps[:, lanes(b)].astype(F32)
        return k[0:8], k[8:16], k[16:24], k[24:32]

    def pool(b):
        k0, k1, k2, k3 = tap_parts(b)
        for p in range(16):
            t = tokv[p * 16 : p * 16 + 16, lanes(b)].astype(F32)
            lo, hi = t[0:8], t[8:16]
            cen[b, p : p + 1] = jnp.sum(lo * k1 + hi * k2, axis=0, keepdims=True)
            up[b, p + 1 : p + 2] = jnp.sum(hi * k0, axis=0, keepdims=True)
            dn[b, p : p + 1] = jnp.sum(lo * k3, axis=0, keepdims=True)
        halo_out[0, b] = dn[b, 0:1]
        halo_out[1, b] = up[b, 16:17]

    loop(0, NB, pool)
    left, right = lax.rem(me + 31, 32), lax.rem(me + 1, 32)

    def halo(k, j, dev):
        return remote(halo_out.at[k], halo_in.at[k], halo_s.at[k], halo_r.at[k], in_seq(dev))

    def halo_pair(k):
        return halo(k, 0, left), halo(k + 1, 1, right)

    def tok_halo(k, dev):
        rows = pl.ds(240 * k, 16)
        return remote(tokens.at[rows, :], tokh.at[k], th_s.at[k], th_r.at[k], in_seq(dev))

    pl.semaphore_wait(barrier, 59)
    to_left, to_right = halo_pair(0)
    to_left.start()
    to_right.start()
    loop(0, EARLY, send_tile)
    to_left.wait()
    to_right.wait()
    first = jnp.where(me == 0, 0.0, 1.0)
    last = jnp.where(me == 31, 0.0, 1.0)

    def finish_pool(b, total):
        up[b, 0:1] = halo_in[1, b] * first
        dn[b, 16:17] = halo_in[0, b] * last
        v = cen[b] + up[b, 0:16] + dn[b, 1:17]
        cen[b] = v
        return total + v * v

    squares = lax.fori_loop(0, NB, finish_pool, jnp.zeros((16, 128), F32))
    inv = lax.rsqrt(jnp.sum(squares, axis=1, keepdims=True) / (NB * 128.0) + 1e-6)
    for c in local[2:5]:
        c.wait()

    def project(b, total):
        n = (cen[b] * inv * gain[lanes(b)].reshape(1, 128)).astype(BF16)
        normed[b] = n
        return total + dot(n, wcat[pl.ds(pl.multiple_of(b * 128, 128), 128), :], 1, 0)

    feats[me] = lax.fori_loop(0, NB, project, jnp.zeros((16, 256), F32)).astype(BF16)

    def feat_copy(slot, dev):
        return remote(feats.at[me], feats.at[me], feat_s.at[slot], feat_r.at[me], in_seq(dev))

    def feat_arrived(k):
        remote(feats.at[k], feats.at[k], feat_s.at[31], feat_r.at[k], in_seq(k)).wait_recv()

    def send_feat(s):
        feat_copy(s, source(s)).start()
        feat_copy(15 + s, target(s)).start()

    feat_copy(30, partner).start()
    loop(0, 15, send_feat)
    loop(EARLY, 15, send_tile)
    tile_copy(15, 0, partner).start()
    tile_copy(15, 1, partner).start()
    tok_halo(0, left).start()
    tok_halo(1, right).start()

    def n_copy(g):
        return remote(normed.at[lax.rem(g, NB)], nin.at[mine], n_s.at[g], n_r.at[mine], owner(g))

    def arrived(buf, sems, k):
        remote(buf.at[k], buf.at[k], n_s.at[0], sems.at[k], owner(k)).wait_recv()

    def others(lo, hi, f):
        @pl.when(lo < hi)
        def _():
            loop(lo, jnp.clip(mine, lo, hi), f)
            loop(jnp.clip(mine + 1, lo, hi), hi, f)

    others(0, 24, lambda g: n_copy(g).start())

    for c in local[5:]:
        c.wait()

    def add_left_right(grad, f):
        accl[...] += grad * f[:, 128:][None]
        accr[...] += grad * f[:, :128][None]

    def tile(s, k, weight):
        own = jnp.concatenate(
            [pairv[:, cols(k), :].reshape(256, 128), cotv[:, cols(k), :].reshape(256, 128)], axis=1
        )
        other = jnp.concatenate([recv[s, 0].reshape(256, 128), recv[s, 1].reshape(256, 128)], axis=1)
        both = own.astype(F32) + dot(perm[...], other, 1, 0)
        here, theirs = feats[me].astype(F32), feats[k].astype(F32)
        outer = here[:, None, :128] * theirs[None, :, 128:] + here[:, None, 128:] * theirs[None, :, :128]
        sym = (both[:, :128] + outer.reshape(256, 128)).astype(BF16)
        cs = both[:, 128:]
        csb = cs.astype(BF16)
        pre = dot(sym, wa[...], 1, 0)
        sig = 0.5 * jnp.tanh(0.5 * pre) + 0.5
        act = pre * sig
        gpre = (dot(csb, wb[...], 1, 1) * (sig + act * (1.0 - sig))).astype(BF16)
        grad = cs + dot(gpre, wa[...], 1, 1)
        wacc[0] += dot(sym, gpre, 0, 0) * weight
        wacc[1] += dot(csb, act.astype(BF16), 0, 0) * weight
        add_left_right(grad.reshape(16, 16, 128), theirs)
        gradb = grad.astype(BF16)
        gpair[:, cols(k), :] = gradb.reshape(16, 16, 128)
        return gradb

    tile(16, me, 0.5)
    tile_copy(15, 0, partner).wait()
    tile_copy(15, 1, partner).wait()
    feat_arrived(partner)
    tile(15, partner, 0.5)

    def ret_copy(s, dev):
        return remote(rbuf.at[s], gpair.at[:, cols(me), :], ret_s.at[s], ret_r.at[s], in_seq(dev))

    def owned(s):
        k = source(s)
        dev = target(s)
        feat_arrived(k)
        tile_copy(s, 0, dev).wait_recv()
        tile_copy(s, 1, dev).wait_recv()
        gradb = tile(s, k, 1.0)
        rbuf[s] = dot(perm[...], gradb, 1, 0).astype(BF16).reshape(16, 16, 128)
        ret_copy(s, k).start()

    loop(0, 15, owned)

    for q in range(4):
        lane = slice(q * 128, q * 128 + 128)
        w3_out[q] = (wacc[0, :, lane] * scale).reshape(8, 16, 128).astype(BF16)
        w3_out[4 + q] = (wacc[1, :, lane].T * scale).reshape(8, 16, 128).astype(BF16)

    def w3_copy(g):
        return remote(w3_out.at[g - 24], w3_in.at[mine], w3_s.at[g - 24], w3_r.at[mine], owner(g))

    others(24, 32, lambda g: w3_copy(g).start())

    def returned(s):
        k = target(s)
        feat_arrived(k)
        remote(rbuf.at[s], gpair.at[:, cols(k), :], ret_s.at[s], ret_r.at[s], in_seq(k)).wait_recv()
        add_left_right(gpair[:, cols(k), :].astype(F32), feats[k].astype(F32))

    loop(0, 15, returned)
    pair_out = pltpu.make_async_copy(gpair, g_pair, loc.at[11])
    pair_out.start()

    glr_out[0] = jnp.sum(accl[...], axis=1).astype(BF16)
    glr_out[1] = jnp.sum(accr[...], axis=1).astype(BF16)

    def g_copy(g):
        return remote(glr_out.at[lax.div(g, NB)], gin.at[mine], g_s.at[g], g_r.at[mine], owner(g))

    others(0, 24, lambda g: g_copy(g).start())
    glr = jnp.concatenate([glr_out[0], glr_out[1]], axis=1)

    def grad_norm(b, carry):
        total, unused = carry
        gn = dot(glr, wcat[pl.ds(pl.multiple_of(b * 128, 128), 128), :], 1, 1)
        scaled = gn * gain[lanes(b)].reshape(1, 128)
        gpx[b, 1:17] = scaled
        mid[8, pl.ds(b, 1)] = jnp.sum(gn * cen[b] * inv, axis=0, keepdims=True) * scale
        return total + scaled * cen[b], unused

    mid[8] = jnp.zeros((16, 128), F32)
    total, _ = lax.fori_loop(0, NB, grad_norm, (jnp.zeros((16, 128), F32), 0))
    mean = jnp.sum(total, axis=1, keepdims=True) / (NB * 128.0) * inv * inv * inv

    def grad_pool(b):
        v = (gpx[b, 1:17] * inv - cen[b] * mean).astype(BF16).astype(F32)
        gpx[b, 1:17] = v
        halo_out[2, b] = v[0:1]
        halo_out[3, b] = v[15:16]

    loop(0, NB, grad_pool)
    to_left2, to_right2 = halo_pair(2)
    to_left2.start()
    to_right2.start()

    w2_out[24] = mid[8].astype(BF16)
    for g in range(25, 32):
        w2_out[g] = jnp.zeros((16, 128), BF16)
    tok_halo(0, left).wait_recv()
    tok_halo(1, right).wait_recv()

    def taps_grad(b):
        s0 = s1 = s2 = s3 = jnp.zeros((8, 128), F32)
        hi_before = tokh[1, :, lanes(b)].astype(F32)[8:16] * first
        t = tokv[0:16, lanes(b)].astype(F32)
        for p in range(16):
            here = gpx[b, p + 1 : p + 2]
            lo, hi = t[0:8], t[8:16]
            if p < 15:
                t = tokv[p * 16 + 16 : p * 16 + 32, lanes(b)].astype(F32)
                lo_after = t[0:8]
            else:
                lo_after = tokh[0, :, lanes(b)].astype(F32)[0:8] * last
            s0 = s0 + here * hi_before
            s1 = s1 + here * lo
            s2 = s2 + here * hi
            s3 = s3 + here * lo_after
            hi_before = hi
        w2_out[2 * b] = (jnp.concatenate([s0, s1], axis=0) * scale).astype(BF16)
        w2_out[2 * b + 1] = (jnp.concatenate([s2, s3], axis=0) * scale).astype(BF16)

    loop(0, NB, taps_grad)

    def w2_copy(g):
        return remote(w2_out.at[g], w2_in.at[mine], w2_s.at[g], w2_r.at[mine], owner(g))

    others(0, 32, lambda g: w2_copy(g).start())

    @pl.when(mine < 24)
    def _():
        others(0, 32, lambda k: arrived(nin, n_r, k))
        nin[mine] = normed[lax.rem(mine, NB)]
        others(0, 32, lambda k: arrived(gin, g_r, k))
        gin[mine] = glr_out[lax.div(mine, NB)]
        prod = dot(nin[...].reshape(512, 128), gin[...].reshape(512, 128), 0, 0) * scale
        mid[0:8] = prod.reshape(8, 16, 128)

    @pl.when(mine >= 24)
    def _():
        others(0, 32, lambda k: arrived(w3_in, w3_r, k))
        w3_in[mine] = w3_out[jnp.maximum(mine - 24, 0)]
        mid[0:8] = lax.fori_loop(1, 32, lambda k, t: t + w3_in[k].astype(F32), w3_in[0].astype(F32))

    others(0, 32, lambda k: arrived(w2_in, w2_r, k))
    w2_in[mine] = w2_out[mine]
    mid[8] = lax.fori_loop(1, 32, lambda k, t: t + w2_in[k].astype(F32), w2_in[0].astype(F32))

    def c_copy(t, dev, slot):
        return (
            remote(mid.at[t], recv_c.at[slot, 0], c_s.at[t, 0], c_r.at[slot, 0], dev),
            remote(mid.at[8], recv_c.at[slot, 1], c_s.at[t, 1], c_r.at[slot, 1], dev),
        )

    def to_ring(v):
        t, dev = ring(v)
        for c in c_copy(t, dev, zz):
            c.start()

    loop(1, 8, to_ring)
    recv_c[zz, 0] = mid[zz]
    recv_c[zz, 1] = mid[8]

    to_left2.wait()
    to_right2.wait()

    def token_grad(b):
        k0, k1, k2, k3 = tap_parts(b)
        gpx[b, 0:1] = halo_in[3, b] * first
        gpx[b, 17:18] = halo_in[2, b] * last
        for p in range(16):
            before, here, after = gpx[b, p : p + 1], gpx[b, p + 1 : p + 2], gpx[b, p + 2 : p + 3]
            g = jnp.concatenate([here * k1 + before * k3, here * k2 + after * k0], axis=0)
            gtokv[p * 16 : p * 16 + 16, lanes(b)] = g.astype(BF16)

    loop(0, NB, token_grad)
    tok_out = pltpu.make_async_copy(gtokv, g_tokens, loc.at[12])
    tok_out.start()

    def from_ring(v):
        t, dev = ring(v)
        for c in c_copy(t, dev, t):
            c.wait_recv()

    loop(1, 8, from_ring)
    summed = recv_c[0]
    for t in range(1, 8):
        summed = summed + recv_c[t]
    fin[zz] = summed[0].astype(BF16)
    fin[8] = summed[1].astype(BF16)

    def f_copy(slot, v, dev):
        return remote(fin.at[slot], fin.at[slot], f_s.at[v], f_r.at[slot], dev)

    loop(1, 8, lambda v: f_copy(zz, v, ring(v)[1]).start())
    loop(1, 8, lambda v: f_copy(ring(v)[0], v, ring(v)[1]).wait_recv())

    def d_copy(u, dev, g):
        return remote(fin, gat.at[g], d_s.at[u], d_r.at[u], dev)

    loop(1, 16, lambda u: d_copy(u, plane(u)[1], mine).start())
    own = pltpu.make_async_copy(fin, gat.at[mine], loc.at[13])
    own.start()
    own.wait()

    def e_copy(u, g):
        return remote(gat.at[g], gat.at[g], e_s.at[u], e_r.at[u], in_seq(partner))

    e_copy(0, mine).start()

    def back(u):
        px, py = lax.rem(x + 4 - lax.div(u, 4), 4), lax.rem(y + 4 - lax.rem(u, 4), 4)
        return px, py

    def forward(u):
        px, py = back(u)
        g = chunk_of(px, py, core)
        d_copy(u, plane(u)[1], g).wait_recv()
        e_copy(u, g).start()

    loop(1, 16, forward)

    def finish(u):
        px, py = back(u)
        e_copy(u, chunk_of(px, py, 1 - core)).wait_recv()

    loop(0, 16, finish)

    def drain_tile(s):
        dev = target(s)
        tile_copy(s, 0, dev).wait_send()
        tile_copy(s, 1, dev).wait_send()
        feat_copy(s, source(s)).wait_send()
        feat_copy(15 + s, dev).wait_send()
        ret_copy(s, source(s)).wait_send()

    loop(0, 15, drain_tile)
    pair_out.wait()
    tok_out.wait()
    feat_copy(30, partner).wait_send()
    tok_halo(0, left).wait_send()
    tok_halo(1, right).wait_send()

    def drain_features(g):
        n_copy(g).wait_send()
        g_copy(g).wait_send()

    others(0, 24, drain_features)
    others(24, 32, lambda g: w3_copy(g).wait_send())
    others(0, 32, lambda g: w2_copy(g).wait_send())
    loop(1, 16, lambda u: d_copy(u, plane(u)[1], mine).wait_send())

    def drain_forward(u):
        px, py = back(u)
        e_copy(u, chunk_of(px, py, core)).wait_send()

    loop(0, 16, drain_forward)

    def drain_ring(v):
        t, dev = ring(v)
        for c in c_copy(t, dev, zz):
            c.wait_send()
        f_copy(zz, v, dev).wait_send()

    loop(1, 8, drain_ring)


def finish(tok_h, pair_h, gat_h, g_tokens, g_pair, g_lw, g_rw, g_taps, g_gain, g_wa, g_wb, pairv, tokv, gat, lwv, rwv, tapsv, gainv, wav, wbv, sem):
    def put(src, dst, k):
        c = pltpu.make_async_copy(src, dst, sem.at[k])
        c.start()
        return c

    weights = put(gat_h, gat, 8)
    parts = [put(pair_h.at[pl.ds(4 * q, 4)], pairv.at[pl.ds(4 * q, 4)], 9 + q) for q in range(4)]
    toks = put(tok_h, tokv, 13)
    weights.wait()
    copies = []
    for b in range(NB):
        rows = slice(b * 128, b * 128 + 128)
        lwv[rows, :] = gat[b, 0:8].reshape(128, 128).astype(F32)
        rwv[rows, :] = gat[b + 12, 0:8].reshape(128, 128).astype(F32)
    copies += [put(lwv, g_lw, 2), put(rwv, g_rw, 3)]
    for q in range(4):
        lane = slice(q * 128, q * 128 + 128)
        wav[:, lane] = gat[24 + q, 0:8].reshape(128, 128).astype(F32)
        wbv[lane, :] = gat[28 + q, 0:8].reshape(128, 128).astype(F32)
    copies += [put(wav, g_wa, 4), put(wbv, g_wb, 5)]
    gains = gat[24, 8].astype(F32)
    for b in range(NB):
        rows = slice(b * 128, b * 128 + 128)
        tapsv[0:16, rows] = gat[2 * b, 8].astype(F32)
        tapsv[16:32, rows] = gat[2 * b + 1, 8].astype(F32)
        gainv[rows] = gains[b]
    copies += [put(tapsv, g_taps, 6), put(gainv, g_gain, 7)]
    for q in range(4):
        parts[q].wait()
        copies.append(put(pairv.at[pl.ds(4 * q, 4)], g_pair.at[pl.ds(4 * q, 4)], 14 + q))
    toks.wait()
    copies.append(put(tokv, g_tokens, 1))
    for c in copies:
        c.wait()


def local(tokens, pair_in, cotangent, kernel, norm_gain, left_weight, right_weight, transition_a, transition_b):
    plen = pair_in.shape[2]
    scale = 1.0 / math.sqrt(lax.axis_size("dp") * plen * plen)
    hbm = pl.BlockSpec(memory_space=pltpu.HBM)
    dma = pltpu.SemaphoreType.DMA
    tile = (16, 16, 128)
    chunk = (9, 16, 128)
    held = pl.pallas_call(
        functools.partial(body, scale),
        out_shape=(
            jax.ShapeDtypeStruct((256, 1536), BF16),
            jax.ShapeDtypeStruct((16, 512, 128), BF16),
            jax.ShapeDtypeStruct((32,) + chunk, BF16),
        ),
        in_specs=[hbm] * 9,
        out_specs=(hbm,) * 3,
        scratch_shapes=[
            pltpu.VMEM((256, 1536), BF16),
            pltpu.VMEM((16, 512, 128), BF16),
            pltpu.VMEM((256, 1536), BF16),
            pltpu.VMEM((2, 16, 1536), BF16),
            pltpu.VMEM((16, 512, 128), BF16),
            pltpu.VMEM((16, 512, 128), BF16),
            pltpu.VMEM((17, 2) + tile, BF16),
            pltpu.VMEM((15,) + tile, BF16),
            pltpu.VMEM((32, 16, 256), BF16),
            pltpu.VMEM((256, 256), BF16),
            pltpu.VMEM((1536, 256), BF16),
            pltpu.VMEM((32, 1536), BF16),
            pltpu.VMEM((1536,), F32),
            pltpu.VMEM((128, 512), BF16),
            pltpu.VMEM((512, 128), BF16),
            pltpu.VMEM((NB, 16, 128), F32),
            pltpu.VMEM((NB, 24, 128), F32),
            pltpu.VMEM((NB, 24, 128), F32),
            pltpu.VMEM((NB, 16, 128), BF16),
            pltpu.VMEM((NB, 24, 128), F32),
            pltpu.VMEM((4, NB, 1, 128), F32),
            pltpu.VMEM((4, NB, 1, 128), F32),
            pltpu.VMEM(tile, F32),
            pltpu.VMEM(tile, F32),
            pltpu.VMEM((2, 128, 512), F32),
            pltpu.VMEM((2, 16, 128), BF16),
            pltpu.VMEM((32, 16, 128), BF16),
            pltpu.VMEM((32, 16, 128), BF16),
            pltpu.VMEM((8, 8, 16, 128), BF16),
            pltpu.VMEM((32, 8, 16, 128), BF16),
            pltpu.VMEM((32, 16, 128), BF16),
            pltpu.VMEM((32, 16, 128), BF16),
            pltpu.VMEM(chunk, F32),
            pltpu.VMEM((8, 2, 16, 128), F32),
            pltpu.VMEM(chunk, BF16),
            dma((14,)),
            dma((16, 2)),
            dma((16, 2)),
            dma((32,)),
            dma((32,)),
            dma((15,)),
            dma((15,)),
            dma((4,)),
            dma((4,)),
            dma((2,)),
            dma((2,)),
            dma((24,)),
            dma((32,)),
            dma((24,)),
            dma((32,)),
            dma((8,)),
            dma((32,)),
            dma((32,)),
            dma((32,)),
            dma((8, 2)),
            dma((8, 2)),
            dma((8,)),
            dma((8,)),
            dma((16,)),
            dma((16,)),
            dma((16,)),
            dma((16,)),
        ],
        compiler_params=pltpu.CompilerParams(
            collective_id=0, has_side_effects=True, vmem_limit_bytes=VMEM_LIMIT
        ),
    )(
        tokens[0],
        pair_in[0],
        cotangent[0],
        kernel,
        norm_gain,
        left_weight,
        right_weight,
        transition_a,
        transition_b,
    )
    outs = pl.pallas_call(
        finish,
        out_shape=(
            jax.ShapeDtypeStruct((256, 1536), BF16),
            jax.ShapeDtypeStruct((16, 512, 128), BF16),
            jax.ShapeDtypeStruct((1536, 128), F32),
            jax.ShapeDtypeStruct((1536, 128), F32),
            jax.ShapeDtypeStruct((32, 1536), F32),
            jax.ShapeDtypeStruct((1536,), F32),
            jax.ShapeDtypeStruct((128, 512), F32),
            jax.ShapeDtypeStruct((512, 128), F32),
        ),
        in_specs=[hbm] * 3,
        out_specs=(hbm,) * 8,
        scratch_shapes=[
            pltpu.VMEM((16, 512, 128), BF16),
            pltpu.VMEM((256, 1536), BF16),
            pltpu.VMEM((32,) + chunk, BF16),
            pltpu.VMEM((1536, 128), F32),
            pltpu.VMEM((1536, 128), F32),
            pltpu.VMEM((32, 1536), F32),
            pltpu.VMEM((1536,), F32),
            pltpu.VMEM((128, 512), F32),
            pltpu.VMEM((512, 128), F32),
            dma((18,)),
        ],
        compiler_params=pltpu.CompilerParams(vmem_limit_bytes=VMEM_LIMIT),
    )(*held)
    return (outs[0][None], outs[1][None], outs[2], outs[3], outs[4], outs[5], outs[6], outs[7])


def solution(mesh):
    placed = (
        P("dp", "seq", None),
        P("dp", "seq", None, None),
        P("dp", "seq", None, None),
        P(),
        P(),
        P(),
        P(),
        P(),
        P(),
    )
    return jax.shard_map(
        local,
        mesh=mesh,
        in_specs=placed,
        out_specs=(P("dp", "seq", None), P("dp", "seq", None, None), P(), P(), P(), P(), P(), P()),
        check_vma=False,
    )
```

time: 149 us -> 130 us (0.87)
  local copies, waits for them, and re-layouts: 14.4 us -> 0 us
  Pallas kernels: 133 us -> 130 us
    unnamed x19 -> x0, local copies, waits for them, and re-layouts: 13.7 us -> none
    pallas_call x1, Pallas kernels: 133 us -> 126 us  [local(): pl.pallas_call(functools.partial(body, scale), out_shape=(jax.ShapeDtypeS...]
    pallas_call x0 -> x1, Pallas kernels: none -> 3.81 us  [local(): pl.pallas_call(finish, out_shape=(jax.ShapeDtypeStruct((256, 1536), BF16)...]
where the time goes in v2:
time: 130 us
  Pallas kernels  130 us (100%)
    pallas_call x1, Pallas kernels, local(): pl.pallas_call(functools.partial(body, scale), out_shape=(jax.ShapeDtypeS...  126 us
    pallas_call x1, Pallas kernels, local(): pl.pallas_call(finish, out_shape=(jax.ShapeDtypeStruct((256, 1536), BF16)...  3.81 us

profile of v2, /device:TPU:1, one launch (start us, length us, event | category | flops | bytes accessed | tf_op | source)
XLA Modules:
  0.0 130.2 jit_solution(12371666200376870061)
XLA Ops:
  0.6 125.7 %shard_map.152 = (bf16[256,1536]{1,0:T(8,128)(2,1)}, bf16[16,512,128]{2,1,0:T(8,128)(2,1)}, bf16[32,9,16,128]{3,2,1,0:T(8,128)(2,1)}) custom-call(bf16[256,1536]{1,0:T(8,128)(2,1)} %bitcast.7, bf16[16,512,128]{2,1,0:T(8,128)(2,1)} %bitcast.5, bf16[16,512,128]{2,1,0:T(8,128)(2,1)} %bitcast.6, bf16[32,1536]{1,0:T(8,128)(2,1)} %taps_h.1, f32[1536]{0:T(1024)} %gain_h.1, ...), custom_call_target="tpu_custom_call" | custom-call | tf_op jit(solution)/shard_map/pallas_call | solution.py:631
  126.4 3.8 %shard_map.153 = (bf16[256,1536]{1,0:T(8,128)(2,1)}, bf16[16,512,128]{2,1,0:T(8,128)(2,1)}, f32[1536,128]{1,0:T(8,128)}, f32[1536,128]{1,0:T(8,128)}, f32[32,153...) custom-call(bf16[256,1536]{1,0:T(8,128)(2,1)} %get-tuple-element.19.tok_h, ...), custom_call_target="tpu_custom_call" | custom-call | tf_op jit(solution)/shard_map/pallas_call | solution.py:718

commit v3 on v2

--- a/solution.py
+++ b/solution.py
@@ -10,7 +10,8 @@
 
 POOL = 16
 NB = 12
-EARLY = 2
+EARLY = 3
+AHEAD = 15
 VMEM_LIMIT = 58 * 1024 * 1024
 F32 = jnp.float32
 BF16 = jnp.bfloat16
@@ -68,6 +69,7 @@
     w2_out,
     w2_in,
     mid,
+    ring_out,
     recv_c,
     fin,
     loc,
@@ -107,10 +109,7 @@
     partner = chip * 2 + 1 - core
 
     def step(s):
-        late = s >= 12
-        dy = jnp.where(late, s - 11, lax.div(s, 3))
-        dz = jnp.where(late, 0, 1 + lax.rem(s + 1, 3))
-        return dy, dz
+        return lax.div(s + 1, 4), lax.rem(s + 1, 4)
 
     def target(s):
         dy, dz = step(s)
@@ -155,6 +154,9 @@
 
     def cols(k):
         return pl.ds(pl.multiple_of(k * 16, 16), 16)
+
+    def fidx(k):
+        return lax.rem(k, 2) * 16 + lax.div(k, 2)
 
     def loop(lo, hi, f):
         def g(i, carry):
@@ -276,21 +278,23 @@
         normed[b] = n
         return total + dot(n, wcat[pl.ds(pl.multiple_of(b * 128, 128), 128), :], 1, 0)
 
-    feats[me] = lax.fori_loop(0, NB, project, jnp.zeros((16, 256), F32)).astype(BF16)
-
-    def feat_copy(slot, dev):
-        return remote(feats.at[me], feats.at[me], feat_s.at[slot], feat_r.at[me], in_seq(dev))
-
-    def feat_arrived(k):
-        remote(feats.at[k], feats.at[k], feat_s.at[31], feat_r.at[k], in_seq(k)).wait_recv()
-
-    def send_feat(s):
-        feat_copy(s, source(s)).start()
-        feat_copy(15 + s, target(s)).start()
-
-    feat_copy(30, partner).start()
-    loop(0, 15, send_feat)
-    loop(EARLY, 15, send_tile)
+    feats[fidx(me)] = lax.fori_loop(0, NB, project, jnp.zeros((16, 256), F32)).astype(BF16)
+
+    def hop1(v):
+        block = feats.at[fidx(me)]
+        return remote(block, block, feat_s.at[v], feat_r.at[v], in_seq(y * 8 + lax.rem(zl + v, 4) * 2 + core))
+
+    def hop2(v):
+        block = feats.at[pl.ds(core * 16 + y * 4, 4)]
+        return remote(block, block, feat_s.at[3 + v], feat_r.at[3 + v], in_seq(lax.rem(y + v, 4) * 8 + zl * 2 + core))
+
+    def hop3(half):
+        block = feats.at[pl.ds(half * 16, 16)]
+        return remote(block, block, feat_s.at[0], feat_r.at[0], in_seq(partner))
+
+    for v in (1, 2, 3):
+        hop1(v).start()
+    loop(EARLY, AHEAD, send_tile)
     tile_copy(15, 0, partner).start()
     tile_copy(15, 1, partner).start()
     tok_halo(0, left).start()
@@ -309,6 +313,10 @@
             loop(jnp.clip(mine + 1, lo, hi), hi, f)
 
     others(0, 24, lambda g: n_copy(g).start())
+    for v in (1, 2, 3):
+        hop1(v).wait_recv()
+    for v in (1, 2, 3):
+        hop2(v).start()
 
     for c in local[5:]:
         c.wait()
@@ -323,7 +331,7 @@
         )
         other = jnp.concatenate([recv[s, 0].reshape(256, 128), recv[s, 1].reshape(256, 128)], axis=1)
         both = own.astype(F32) + dot(perm[...], other, 1, 0)
-        here, theirs = feats[me].astype(F32), feats[k].astype(F32)
+        here, theirs = feats[fidx(me)].astype(F32), feats[fidx(k)].astype(F32)
         outer = here[:, None, :128] * theirs[None, :, 128:] + here[:, None, 128:] * theirs[None, :, :128]
         sym = (both[:, :128] + outer.reshape(256, 128)).astype(BF16)
         cs = both[:, 128:]
@@ -341,18 +349,21 @@
         return gradb
 
     tile(16, me, 0.5)
+    for v in (1, 2, 3):
+        hop2(v).wait_recv()
+    hop3(core).start()
     tile_copy(15, 0, partner).wait()
     tile_copy(15, 1, partner).wait()
-    feat_arrived(partner)
+    hop3(1 - core).wait_recv()
     tile(15, partner, 0.5)
 
     def ret_copy(s, dev):
         return remote(rbuf.at[s], gpair.at[:, cols(me), :], ret_s.at[s], ret_r.at[s], in_seq(dev))
 
     def owned(s):
+        pl.when(s + AHEAD < 15)(lambda: send_tile(s + AHEAD))
         k = source(s)
         dev = target(s)
-        feat_arrived(k)
         tile_copy(s, 0, dev).wait_recv()
         tile_copy(s, 1, dev).wait_recv()
         gradb = tile(s, k, 1.0)
@@ -373,9 +384,8 @@
 
     def returned(s):
         k = target(s)
-        feat_arrived(k)
         remote(rbuf.at[s], gpair.at[:, cols(k), :], ret_s.at[s], ret_r.at[s], in_seq(k)).wait_recv()
-        add_left_right(gpair[:, cols(k), :].astype(F32), feats[k].astype(F32))
+        add_left_right(gpair[:, cols(k), :].astype(F32), feats[fidx(k)].astype(F32))
 
     loop(0, 15, returned)
     pair_out = pltpu.make_async_copy(gpair, g_pair, loc.at[11])
@@ -461,25 +471,51 @@
         w3_in[mine] = w3_out[jnp.maximum(mine - 24, 0)]
         mid[0:8] = lax.fori_loop(1, 32, lambda k, t: t + w3_in[k].astype(F32), w3_in[0].astype(F32))
 
+    def c_copy(t, dev, slot):
+        return remote(ring_out.at[t], recv_c.at[slot, 0], c_s.at[t, 0], c_r.at[slot, 0], dev)
+
+    def c2_copy(t, dev, slot):
+        return remote(ring_out.at[8], recv_c.at[slot, 1], c_s.at[t, 1], c_r.at[slot, 1], dev)
+
+    def f_copy(slot, v, dev):
+        return remote(fin.at[slot], fin.at[slot], f_s.at[v], f_r.at[slot], dev)
+
+    def on_ring(f):
+        loop(1, 8, lambda v: f(v, *ring(v)))
+
+    ring_out[0:8] = mid[0:8].astype(BF16)
+    on_ring(lambda v, t, dev: c_copy(t, dev, zz).start())
+    recv_c[zz, 0] = ring_out[zz]
+
     others(0, 32, lambda k: arrived(w2_in, w2_r, k))
     w2_in[mine] = w2_out[mine]
-    mid[8] = lax.fori_loop(1, 32, lambda k, t: t + w2_in[k].astype(F32), w2_in[0].astype(F32))
-
-    def c_copy(t, dev, slot):
-        return (
-            remote(mid.at[t], recv_c.at[slot, 0], c_s.at[t, 0], c_r.at[slot, 0], dev),
-            remote(mid.at[8], recv_c.at[slot, 1], c_s.at[t, 1], c_r.at[slot, 1], dev),
-        )
-
-    def to_ring(v):
-        t, dev = ring(v)
-        for c in c_copy(t, dev, zz):
-            c.start()
-
-    loop(1, 8, to_ring)
-    recv_c[zz, 0] = mid[zz]
-    recv_c[zz, 1] = mid[8]
-
+    summed = lax.fori_loop(1, 32, lambda k, t: t + w2_in[k].astype(F32), w2_in[0].astype(F32))
+    ring_out[8] = summed.astype(BF16)
+    on_ring(lambda v, t, dev: c2_copy(t, dev, zz).start())
+    recv_c[zz, 1] = ring_out[8]
+
+    def ring_sum(k):
+        return lax.fori_loop(1, 8, lambda t, a: a + recv_c[t, k].astype(F32), recv_c[0, k].astype(F32))
+
+    on_ring(lambda v, t, dev: c_copy(t, dev, t).wait_recv())
+    fin[zz] = ring_sum(0).astype(BF16)
+    on_ring(lambda v, t, dev: f_copy(zz, v, dev).start())
+    on_ring(lambda v, t, dev: c2_copy(t, dev, t).wait_recv())
+    fin[8] = ring_sum(1).astype(BF16)
+    on_ring(lambda v, t, dev: f_copy(t, v, dev).wait_recv())
+
+    def d_copy(u, dev, g):
+        return remote(fin, gat.at[g], d_s.at[u], d_r.at[u], dev)
+
+    loop(1, 16, lambda u: d_copy(u, plane(u)[1], mine).start())
+    own = pltpu.make_async_copy(fin, gat.at[mine], loc.at[13])
+    own.start()
+    own.wait()
+
+    def e_copy(u, g):
+        return remote(gat.at[g], gat.at[g], e_s.at[u], e_r.at[u], in_seq(partner))
+
+    e_copy(0, mine).start()
     to_left2.wait()
     to_right2.wait()
 
@@ -496,37 +532,6 @@
     tok_out = pltpu.make_async_copy(gtokv, g_tokens, loc.at[12])
     tok_out.start()
 
-    def from_ring(v):
-        t, dev = ring(v)
-        for c in c_copy(t, dev, t):
-            c.wait_recv()
-
-    loop(1, 8, from_ring)
-    summed = recv_c[0]
-    for t in range(1, 8):
-        summed = summed + recv_c[t]
-    fin[zz] = summed[0].astype(BF16)
-    fin[8] = summed[1].astype(BF16)
-
-    def f_copy(slot, v, dev):
-        return remote(fin.at[slot], fin.at[slot], f_s.at[v], f_r.at[slot], dev)
-
-    loop(1, 8, lambda v: f_copy(zz, v, ring(v)[1]).start())
-    loop(1, 8, lambda v: f_copy(ring(v)[0], v, ring(v)[1]).wait_recv())
-
-    def d_copy(u, dev, g):
-        return remote(fin, gat.at[g], d_s.at[u], d_r.at[u], dev)
-
-    loop(1, 16, lambda u: d_copy(u, plane(u)[1], mine).start())
-    own = pltpu.make_async_copy(fin, gat.at[mine], loc.at[13])
-    own.start()
-    own.wait()
-
-    def e_copy(u, g):
-        return remote(gat.at[g], gat.at[g], e_s.at[u], e_r.at[u], in_seq(partner))
-
-    e_copy(0, mine).start()
-
     def back(u):
         px, py = lax.rem(x + 4 - lax.div(u, 4), 4), lax.rem(y + 4 - lax.rem(u, 4), 4)
         return px, py
@@ -549,14 +554,15 @@
         dev = target(s)
         tile_copy(s, 0, dev).wait_send()
         tile_copy(s, 1, dev).wait_send()
-        feat_copy(s, source(s)).wait_send()
-        feat_copy(15 + s, dev).wait_send()
         ret_copy(s, source(s)).wait_send()
 
     loop(0, 15, drain_tile)
     pair_out.wait()
     tok_out.wait()
-    feat_copy(30, partner).wait_send()
+    for v in (1, 2, 3):
+        hop1(v).wait_send()
+        hop2(v).wait_send()
+    hop3(core).wait_send()
     tok_halo(0, left).wait_send()
     tok_halo(1, right).wait_send()
 
@@ -575,13 +581,12 @@
 
     loop(0, 16, drain_forward)
 
-    def drain_ring(v):
-        t, dev = ring(v)
-        for c in c_copy(t, dev, zz):
-            c.wait_send()
+    def drain_ring(v, t, dev):
+        c_copy(t, dev, zz).wait_send()
+        c2_copy(t, dev, zz).wait_send()
         f_copy(zz, v, dev).wait_send()
 
-    loop(1, 8, drain_ring)
+    on_ring(drain_ring)
 
 
 def finish(tok_h, pair_h, gat_h, g_tokens, g_pair, g_lw, g_rw, g_taps, g_gain, g_wa, g_wb, pairv, tokv, gat, lwv, rwv, tapsv, gainv, wav, wbv, sem):
@@ -671,13 +676,14 @@
             pltpu.VMEM((32, 16, 128), BF16),
             pltpu.VMEM((32, 16, 128), BF16),
             pltpu.VMEM(chunk, F32),
-            pltpu.VMEM((8, 2, 16, 128), F32),
+            pltpu.VMEM(chunk, BF16),
+            pltpu.VMEM((8, 2, 16, 128), BF16),
             pltpu.VMEM(chunk, BF16),
             dma((14,)),
             dma((16, 2)),
             dma((16, 2)),
-            dma((32,)),
-            dma((32,)),
+            dma((7,)),
+            dma((7,)),
             dma((15,)),
             dma((15,)),
             dma((4,)),

time: 130 us -> 119 us (0.915)
  Pallas kernels: 130 us -> 119 us
    pallas_call x1, Pallas kernels: 126 us -> 115 us  [local(): pl.pallas_call(functools.partial(body, scale), out_shape=(jax.ShapeDtypeS...]
where the time goes in v3:
time: 119 us
  Pallas kernels  119 us (100%)
    pallas_call x1, Pallas kernels, local(): pl.pallas_call(functools.partial(body, scale), out_shape=(jax.ShapeDtypeS...  115 us
    pallas_call x1, Pallas kernels, local(): pl.pallas_call(finish, out_shape=(jax.ShapeDtypeStruct((256, 1536), BF16)...  3.81 us

profile of v3, /device:TPU:1, one launch (start us, length us, event | category | flops | bytes accessed | tf_op | source)
XLA Modules:
  0.0 119.3 jit_solution(13852961680884742222)
XLA Ops:
  0.6 114.9 %shard_map.152 = (bf16[256,1536]{1,0:T(8,128)(2,1)}, bf16[16,512,128]{2,1,0:T(8,128)(2,1)}, bf16[32,9,16,128]{3,2,1,0:T(8,128)(2,1)}) custom-call(bf16[256,1536]{1,0:T(8,128)(2,1)} %bitcast.7, bf16[16,512,128]{2,1,0:T(8,128)(2,1)} %bitcast.5, bf16[16,512,128]{2,1,0:T(8,128)(2,1)} %bitcast.6, bf16[32,1536]{1,0:T(8,128)(2,1)} %taps_h.1, f32[1536]{0:T(1024)} %gain_h.1, ...), custom_call_target="tpu_custom_call" | custom-call | tf_op jit(solution)/shard_map/pallas_call | solution.py:636
  115.5 3.8 %shard_map.153 = (bf16[256,1536]{1,0:T(8,128)(2,1)}, bf16[16,512,128]{2,1,0:T(8,128)(2,1)}, f32[1536,128]{1,0:T(8,128)}, f32[1536,128]{1,0:T(8,128)}, f32[32,153...) custom-call(bf16[256,1536]{1,0:T(8,128)(2,1)} %get-tuple-element.19.tok_h, ...), custom_call_target="tpu_custom_call" | custom-call | tf_op jit(solution)/shard_map/pallas_call | solution.py:724

commit v4 on v3

--- a/solution.py
+++ b/solution.py
@@ -10,7 +10,7 @@
 
 POOL = 16
 NB = 12
-EARLY = 3
+EARLY = 7
 AHEAD = 15
 VMEM_LIMIT = 58 * 1024 * 1024
 F32 = jnp.float32
@@ -109,7 +109,7 @@
     partner = chip * 2 + 1 - core
 
     def step(s):
-        return lax.div(s + 1, 4), lax.rem(s + 1, 4)
+        return lax.div(15 - s, 4), lax.rem(15 - s, 4)
 
     def target(s):
         dy, dz = step(s)
@@ -205,7 +205,8 @@
             (pair, cot)[k].at[:, cols(dev), :], recv.at[s, k], tile_s.at[s, k], tile_r.at[s, k], in_seq(dev)
         )
 
-    def send_tile(s):
+    def send_tile(i):
+        s = jnp.where((core == 1) & (i < 14), i + 1 - 2 * lax.rem(i, 2), i)
         dev = target(s)
         tile_copy(s, 0, dev).start()
         tile_copy(s, 1, dev).start()
@@ -382,6 +383,17 @@
 
     others(24, 32, lambda g: w3_copy(g).start())
 
+    @pl.when(mine < 24)
+    def _():
+        others(0, 32, lambda k: arrived(nin, n_r, k))
+        nin[mine] = normed[lax.rem(mine, NB)]
+
+    @pl.when(mine >= 24)
+    def _():
+        others(0, 32, lambda k: arrived(w3_in, w3_r, k))
+        w3_in[mine] = w3_out[jnp.maximum(mine - 24, 0)]
+        mid[0:8] = lax.fori_loop(1, 32, lambda k, t: t + w3_in[k].astype(F32), w3_in[0].astype(F32))
+
     def returned(s):
         k = target(s)
         remote(rbuf.at[s], gpair.at[:, cols(k), :], ret_s.at[s], ret_r.at[s], in_seq(k)).wait_recv()
@@ -458,18 +470,10 @@
 
     @pl.when(mine < 24)
     def _():
-        others(0, 32, lambda k: arrived(nin, n_r, k))
-        nin[mine] = normed[lax.rem(mine, NB)]
         others(0, 32, lambda k: arrived(gin, g_r, k))
         gin[mine] = glr_out[lax.div(mine, NB)]
         prod = dot(nin[...].reshape(512, 128), gin[...].reshape(512, 128), 0, 0) * scale
         mid[0:8] = prod.reshape(8, 16, 128)
-
-    @pl.when(mine >= 24)
-    def _():
-        others(0, 32, lambda k: arrived(w3_in, w3_r, k))
-        w3_in[mine] = w3_out[jnp.maximum(mine - 24, 0)]
-        mid[0:8] = lax.fori_loop(1, 32, lambda k, t: t + w3_in[k].astype(F32), w3_in[0].astype(F32))
 
     def c_copy(t, dev, slot):
         return remote(ring_out.at[t], recv_c.at[slot, 0], c_s.at[t, 0], c_r.at[slot, 0], dev)
@@ -510,12 +514,14 @@
     loop(1, 16, lambda u: d_copy(u, plane(u)[1], mine).start())
     own = pltpu.make_async_copy(fin, gat.at[mine], loc.at[13])
     own.start()
-    own.wait()
 
     def e_copy(u, g):
         return remote(gat.at[g], gat.at[g], e_s.at[u], e_r.at[u], in_seq(partner))
 
-    e_copy(0, mine).start()
+    def e_own(g):
+        return remote(fin, gat.at[g], e_s.at[0], e_r.at[0], in_seq(partner))
+
+    e_own(mine).start()
     to_left2.wait()
     to_right2.wait()
 
@@ -532,24 +538,6 @@
     tok_out = pltpu.make_async_copy(gtokv, g_tokens, loc.at[12])
     tok_out.start()
 
-    def back(u):
-        px, py = lax.rem(x + 4 - lax.div(u, 4), 4), lax.rem(y + 4 - lax.rem(u, 4), 4)
-        return px, py
-
-    def forward(u):
-        px, py = back(u)
-        g = chunk_of(px, py, core)
-        d_copy(u, plane(u)[1], g).wait_recv()
-        e_copy(u, g).start()
-
-    loop(1, 16, forward)
-
-    def finish(u):
-        px, py = back(u)
-        e_copy(u, chunk_of(px, py, 1 - core)).wait_recv()
-
-    loop(0, 16, finish)
-
     def drain_tile(s):
         dev = target(s)
         tile_copy(s, 0, dev).wait_send()
@@ -558,7 +546,6 @@
 
     loop(0, 15, drain_tile)
     pair_out.wait()
-    tok_out.wait()
     for v in (1, 2, 3):
         hop1(v).wait_send()
         hop2(v).wait_send()
@@ -573,20 +560,41 @@
     others(0, 24, drain_features)
     others(24, 32, lambda g: w3_copy(g).wait_send())
     others(0, 32, lambda g: w2_copy(g).wait_send())
-    loop(1, 16, lambda u: d_copy(u, plane(u)[1], mine).wait_send())
-
-    def drain_forward(u):
-        px, py = back(u)
-        e_copy(u, chunk_of(px, py, core)).wait_send()
-
-    loop(0, 16, drain_forward)
-
     def drain_ring(v, t, dev):
         c_copy(t, dev, zz).wait_send()
         c2_copy(t, dev, zz).wait_send()
         f_copy(zz, v, dev).wait_send()
 
     on_ring(drain_ring)
+
+    def back(u):
+        px, py = lax.rem(x + 4 - lax.div(u, 4), 4), lax.rem(y + 4 - lax.rem(u, 4), 4)
+        return px, py
+
+    def forward(u):
+        px, py = back(u)
+        g = chunk_of(px, py, core)
+        d_copy(u, plane(u)[1], g).wait_recv()
+        e_copy(u, g).start()
+
+    loop(1, 16, forward)
+
+    def finish(u):
+        px, py = back(u)
+        e_copy(u, chunk_of(px, py, 1 - core)).wait_recv()
+
+    loop(0, 16, finish)
+
+    own.wait()
+    tok_out.wait()
+    loop(1, 16, lambda u: d_copy(u, plane(u)[1], mine).wait_send())
+
+    def drain_forward(u):
+        px, py = back(u)
+        e_copy(u, chunk_of(px, py, core)).wait_send()
+
+    e_own(mine).wait_send()
+    loop(1, 16, drain_forward)
 
 
 def finish(tok_h, pair_h, gat_h, g_tokens, g_pair, g_lw, g_rw, g_taps, g_gain, g_wa, g_wb, pairv, tokv, gat, lwv, rwv, tapsv, gainv, wav, wbv, sem):
@@ -598,8 +606,13 @@
     weights = put(gat_h, gat, 8)
     parts = [put(pair_h.at[pl.ds(4 * q, 4)], pairv.at[pl.ds(4 * q, 4)], 9 + q) for q in range(4)]
     toks = put(tok_h, tokv, 13)
+    copies = []
+    for q in range(4):
+        parts[q].wait()
+        copies.append(put(pairv.at[pl.ds(4 * q, 4)], g_pair.at[pl.ds(4 * q, 4)], 14 + q))
+    toks.wait()
+    copies.append(put(tokv, g_tokens, 1))
     weights.wait()
-    copies = []
     for b in range(NB):
         rows = slice(b * 128, b * 128 + 128)
         lwv[rows, :] = gat[b, 0:8].reshape(128, 128).astype(F32)
@@ -617,11 +630,6 @@
         tapsv[16:32, rows] = gat[2 * b + 1, 8].astype(F32)
         gainv[rows] = gains[b]
     copies += [put(tapsv, g_taps, 6), put(gainv, g_gain, 7)]
-    for q in range(4):
-        parts[q].wait()
-        copies.append(put(pairv.at[pl.ds(4 * q, 4)], g_pair.at[pl.ds(4 * q, 4)], 14 + q))
-    toks.wait()
-    copies.append(put(tokv, g_tokens, 1))
     for c in copies:
         c.wait()
 

time: 119 us -> 117 us (0.983)
  Pallas kernels: 119 us -> 117 us
    pallas_call x1, Pallas kernels: 115 us -> 113 us  [local(): pl.pallas_call(functools.partial(body, scale), out_shape=(jax.ShapeDtypeS...]
where the time goes in v4:
time: 117 us
  Pallas kernels  117 us (100%)
    pallas_call x1, Pallas kernels, local(): pl.pallas_call(functools.partial(body, scale), out_shape=(jax.ShapeDtypeS...  113 us
    pallas_call x1, Pallas kernels, local(): pl.pallas_call(finish, out_shape=(jax.ShapeDtypeStruct((256, 1536), BF16)...  3.89 us

profile of v4, /device:TPU:1, one launch (start us, length us, event | category | flops | bytes accessed | tf_op | source)
XLA Modules:
  0.0 117.3 jit_solution(10797550566040240325)
XLA Ops:
  0.6 112.8 %shard_map.152 = (bf16[256,1536]{1,0:T(8,128)(2,1)}, bf16[16,512,128]{2,1,0:T(8,128)(2,1)}, bf16[32,9,16,128]{3,2,1,0:T(8,128)(2,1)}) custom-call(bf16[256,1536]{1,0:T(8,128)(2,1)} %bitcast.7, bf16[16,512,128]{2,1,0:T(8,128)(2,1)} %bitcast.5, bf16[16,512,128]{2,1,0:T(8,128)(2,1)} %bitcast.6, bf16[32,1536]{1,0:T(8,128)(2,1)} %taps_h.1, f32[1536]{0:T(1024)} %gain_h.1, ...), custom_call_target="tpu_custom_call" | custom-call | tf_op jit(solution)/shard_map/pallas_call | solution.py:644
  113.4 3.9 %shard_map.153 = (bf16[256,1536]{1,0:T(8,128)(2,1)}, bf16[16,512,128]{2,1,0:T(8,128)(2,1)}, f32[1536,128]{1,0:T(8,128)}, f32[1536,128]{1,0:T(8,128)}, f32[32,153...) custom-call(bf16[256,1536]{1,0:T(8,128)(2,1)} %get-tuple-element.19.tok_h, ...), custom_call_target="tpu_custom_call" | custom-call | tf_op jit(solution)/shard_map/pallas_call | solution.py:732

commit v5 on v4

--- a/solution.py
+++ b/solution.py
@@ -388,12 +388,6 @@
         others(0, 32, lambda k: arrived(nin, n_r, k))
         nin[mine] = normed[lax.rem(mine, NB)]
 
-    @pl.when(mine >= 24)
-    def _():
-        others(0, 32, lambda k: arrived(w3_in, w3_r, k))
-        w3_in[mine] = w3_out[jnp.maximum(mine - 24, 0)]
-        mid[0:8] = lax.fori_loop(1, 32, lambda k, t: t + w3_in[k].astype(F32), w3_in[0].astype(F32))
-
     def returned(s):
         k = target(s)
         remote(rbuf.at[s], gpair.at[:, cols(k), :], ret_s.at[s], ret_r.at[s], in_seq(k)).wait_recv()
@@ -474,6 +468,12 @@
         gin[mine] = glr_out[lax.div(mine, NB)]
         prod = dot(nin[...].reshape(512, 128), gin[...].reshape(512, 128), 0, 0) * scale
         mid[0:8] = prod.reshape(8, 16, 128)
+
+    @pl.when(mine >= 24)
+    def _():
+        others(0, 32, lambda k: arrived(w3_in, w3_r, k))
+        w3_in[mine] = w3_out[jnp.maximum(mine - 24, 0)]
+        mid[0:8] = lax.fori_loop(1, 32, lambda k, t: t + w3_in[k].astype(F32), w3_in[0].astype(F32))
 
     def c_copy(t, dev, slot):
         return remote(ring_out.at[t], recv_c.at[slot, 0], c_s.at[t, 0], c_r.at[slot, 0], dev)

time: 117 us -> 117 us (level)
  no operation moved by 1% of the time
where the time goes in v5:
time: 117 us
  Pallas kernels  117 us (100%)
    pallas_call x1, Pallas kernels, local(): pl.pallas_call(functools.partial(body, scale), out_shape=(jax.ShapeDtypeS...  113 us
    pallas_call x1, Pallas kernels, local(): pl.pallas_call(finish, out_shape=(jax.ShapeDtypeStruct((256, 1536), BF16)...  3.89 us

profile of v5, /device:TPU:1, one launch (start us, length us, event | category | flops | bytes accessed | tf_op | source)
XLA Modules:
  0.0 117.3 jit_solution(4921192608477205666)
XLA Ops:
  0.6 112.8 %shard_map.152 = (bf16[256,1536]{1,0:T(8,128)(2,1)}, bf16[16,512,128]{2,1,0:T(8,128)(2,1)}, bf16[32,9,16,128]{3,2,1,0:T(8,128)(2,1)}) custom-call(bf16[256,1536]{1,0:T(8,128)(2,1)} %bitcast.7, bf16[16,512,128]{2,1,0:T(8,128)(2,1)} %bitcast.5, bf16[16,512,128]{2,1,0:T(8,128)(2,1)} %bitcast.6, bf16[32,1536]{1,0:T(8,128)(2,1)} %taps_h.1, f32[1536]{0:T(1024)} %gain_h.1, ...), custom_call_target="tpu_custom_call" | custom-call | tf_op jit(solution)/shard_map/pallas_call | solution.py:644
  113.4 3.9 %shard_map.153 = (bf16[256,1536]{1,0:T(8,128)(2,1)}, bf16[16,512,128]{2,1,0:T(8,128)(2,1)}, f32[1536,128]{1,0:T(8,128)}, f32[1536,128]{1,0:T(8,128)}, f32[32,153...) custom-call(bf16[256,1536]{1,0:T(8,128)(2,1)} %get-tuple-element.19.tok_h, ...), custom_call_target="tpu_custom_call" | custom-call | tf_op jit(solution)/shard_map/pallas_call | solution.py:732
